TPU v7x, 256 devices: a whole 4x4x8 slice. The times are simulated.
256 devices in a mesh: section: 8 (over y, z_lo), dp: 32 (over z_hi, x, core).
Axes of the slice: x: 4, y: 4, z: 8 (z_hi: 4, z_lo: 2; z = z_hi * 2 + z_lo), core: 2. Of those that a mesh axis runs over, the one named last changes fastest.
Arguments:
- pre_norm: bfloat16 [2, 32, 48, 4096], P(None, 'dp'), may hold values from -12 to 12
- norm_gain: float32 [4096], replicated, may hold values from 0.3 to 3
- queries: bfloat16 [8, 2, 32, 128, 2048], P('section', None, 'dp'), may hold values from -24 to 24
- keys: bfloat16 [8, 2, 32, 48, 2048], P('section', None, 'dp'), may hold values from -6 to 6
- values: bfloat16 [8, 2, 32, 48, 2048], P('section', None, 'dp'), may hold values from -6 to 6
- head_grad: bfloat16 [8, 2, 32, 128, 2048], P('section', None, 'dp'), may hold values from -2 to 2
- key_weight: bfloat16 [8, 4096, 2048], P('section', 'dp'), may hold values from -0.09375 to 0.09375
- value_weight: bfloat16 [8, 4096, 2048], P('section', 'dp'), may hold values from -0.09375 to 0.09375
Outputs:
- query_grad: bfloat16 [8, 2, 32, 128, 2048], P('section', None, 'dp')
- key_weight_grad: bfloat16 [8, 4096, 2048], P('section', 'dp')
- value_weight_grad: bfloat16 [8, 4096, 2048], P('section', 'dp')
- encoder_grad: bfloat16 [2, 32, 48, 4096], P(None, 'dp')
- gain_grad: float32 [4096], replicated
All inputs are finite; a program needn't handle non-finite values.
Results may differ from a plain program's by a relative error of at most 0.02.
Values may be sent and summed in bfloat16 or wider, within the bound.
No kernel may reach another device: no remote copies, remote signals or barrier semaphores. Data moves between devices by JAX's collectives and lax.ppermute only.
A program may use at most 128 MiB of HBM per device.

v0:
```python
import jax
import jax.numpy as jnp
from jax import lax
from jax.sharding import PartitionSpec as P

HEAD_DIM = 64


epsilon = 1e-06


def from_behind(value, axis, steps):
    count = lax.axis_size(axis)
    first, last = (max(0, -steps), min(count, count - steps))
    return lax.ppermute(value, axis, [(source, source + steps) for source in range(first, last)])


def backward_heads(query_rows, key_rows, value_rows, grad_rows):
    batches, target_n, inner = query_rows.shape
    source_n = key_rows.shape[1]
    head_count = inner // HEAD_DIM
    query_h = query_rows.reshape(batches, target_n, head_count, HEAD_DIM)
    key_h = key_rows.reshape(batches, source_n, head_count, HEAD_DIM)
    value_h = value_rows.reshape(batches, source_n, head_count, HEAD_DIM)
    grad_h = grad_rows.reshape(batches, target_n, head_count, HEAD_DIM)
    scores = jnp.einsum("mshe,mthe->mhst", key_h, query_h, preferred_element_type=jnp.float32)
    highest = jnp.max(scores, axis=2, keepdims=True)
    exponent = jnp.exp(scores - highest)
    softmax_w = exponent / jnp.sum(exponent, axis=2, keepdims=True)
    rounded_w = softmax_w.astype(jnp.bfloat16)
    slopes = jnp.einsum("mshe,mthe->mhst", value_h, grad_h, preferred_element_type=jnp.float32)
    center = jnp.sum(softmax_w * slopes, axis=2, keepdims=True)
    score_grad = (softmax_w * (slopes - center)).astype(jnp.bfloat16)
    value_grad = jnp.einsum(
        "mhst,mthe->mshe", rounded_w, grad_h, preferred_element_type=jnp.float32
    )
    key_grad = jnp.einsum(
        "mhst,mthe->mshe", score_grad, query_h, preferred_element_type=jnp.float32
    )
    query_local = jnp.einsum(
        "mhst,mshe->mthe", score_grad, key_h, preferred_element_type=jnp.float32
    )
    return (
        query_local.astype(jnp.bfloat16).reshape(batches, target_n, inner),
        key_grad.astype(jnp.bfloat16).reshape(batches * source_n, inner),
        value_grad.astype(jnp.bfloat16).reshape(batches * source_n, inner),
    )


def make_fold(columns, key_shard, value_shard, pieces):
    key_piece, value_piece = pieces
    grad_key = jnp.einsum("rd,rh->dh", columns, key_piece, preferred_element_type=jnp.float32)
    grad_value = jnp.einsum("rd,rh->dh", columns, value_piece, preferred_element_type=jnp.float32)
    returned_piece = jnp.einsum(
        "rh,dh->rd", key_piece, key_shard, preferred_element_type=jnp.float32
    )
    returned_piece = returned_piece + jnp.einsum(
        "rh,dh->rd", value_piece, value_shard, preferred_element_type=jnp.float32
    )
    return (grad_key, grad_value, returned_piece)


def body(pre_norm, norm_gain, queries, keys, values, head_grad, key_weight, value_weight):
    batches, single_seq, source_n, features = pre_norm.shape
    hidden_f = pre_norm.astype(jnp.float32).reshape(batches * source_n, features)
    inverse = lax.rsqrt(jnp.mean(hidden_f * hidden_f, axis=-1, keepdims=True) + epsilon)
    memory = (hidden_f * inverse * norm_gain).astype(jnp.bfloat16)
    columns = lax.all_to_all(memory, "dp", split_axis=1, concat_axis=0, tiled=True)
    key_shard = key_weight[0]
    value_shard = value_weight[0]
    query_rows = queries[0, :, 0]
    key_rows = keys[0, :, 0]
    value_rows = values[0, :, 0]
    grad_rows = head_grad[0, :, 0]
    query_local, key_grad, value_grad = backward_heads(query_rows, key_rows, value_rows, grad_rows)
    grad_key, grad_value, returned = make_fold(
        columns,
        key_shard,
        value_shard,
        (
            lax.all_gather(key_grad, "dp", axis=0, tiled=True),
            lax.all_gather(value_grad, "dp", axis=0, tiled=True),
        ),
    )
    query_grad = from_behind(query_local.reshape(queries.shape), "section", -1)
    local_grad = lax.all_to_all(
        returned.astype(jnp.bfloat16), "dp", split_axis=0, concat_axis=1, tiled=True
    ).astype(returned.dtype)
    summed = lax.psum(local_grad.astype(jnp.bfloat16), "section").astype(jnp.float32)
    scaled = norm_gain * summed
    row_mean = jnp.mean(hidden_f * scaled, axis=-1, keepdims=True)
    encoder_flat = (inverse * scaled - hidden_f * inverse * inverse * inverse * row_mean).astype(
        jnp.bfloat16
    )
    gain_grad = lax.psum(jnp.sum(summed * hidden_f * inverse, axis=0), "dp")
    encoder_grad = encoder_flat.reshape(pre_norm.shape)
    return (
        query_grad,
        grad_key.astype(jnp.bfloat16)[None],
        grad_value.astype(jnp.bfloat16)[None],
        encoder_grad,
        gain_grad,
    )


def solution(mesh):
    return jax.shard_map(
        body,
        mesh=mesh,
        in_specs=(
            P(None, "dp", None, None),
            P(),
            P("section", None, "dp", None, None),
            P("section", None, "dp", None, None),
            P("section", None, "dp", None, None),
            P("section", None, "dp", None, None),
            P("section", "dp", None),
            P("section", "dp", None),
        ),
        out_specs=(
            P("section", None, "dp", None, None),
            P("section", "dp", None),
            P("section", "dp", None),
            P(None, "dp", None, None),
            P(),
        ),
        check_vma=False,
    )
```

profile of v0, /device:TPU:8, one launch (start us, length us, event | category | flops | bytes accessed | tf_op | source)
XLA Modules:
  0.0 517.4 jit_solution(14680348962406117134)
XLA Ops:
  7.2 1.7 copy.42
  9.0 0.8 reshape_squeeze.12
  9.8 2.3 copy.44
  12.0 0.8 reshape_squeeze.14
  12.9 1.9 fusion.29
  14.7 2.4 multiply_reduce_fusion.1
  17.2 0.4 multiply_convert_fusion
  17.5 0.7 fusion.18
  18.4 1.4 reshape.69
  19.9 2.4 fusion.19
  22.5 1.4 reshape.70
  23.9 97.7 %all-gather.3.cloned.1.call-done = bf16[3072,2048]{1,0:T(8,128)(2,1)} async-done(((bf16[96,2048]{1,0:T(8,128)(2,1)}), bf16[3072,2048]{1,0:T(8,128)(2,1)}) %all-gather.3.cloned.1.call-update) | async-done | bytes 12582928 | tf_op jit(solution)/shard_map/all_gather | solution.py:81
  121.6 7.6 %fusion.27 = f32[3072,128]{1,0:T(8,128)} fusion(bf16[3072,2048]{1,0:T(8,128)(2,1)} %all-gather.3.cloned.1.call-done, bf16[1,128,2048]{2,1,0:T(8,128)(2,1)S(1)} %copy-done), kind=kOutput, calls=%fused_computation.42 | convolution fusion | flops 1610612736 | bytes 14680064 | tf_op jit(solution)/shard_map/rh,dh->rd/dot_general | solution.py:54
  129.2 92.7 %all-gather.5.cloned.1.call-done = bf16[3072,2048]{1,0:T(8,128)(2,1)} async-done(((bf16[96,2048]{1,0:T(8,128)(2,1)}), bf16[3072,2048]{1,0:T(8,128)(2,1)}) %all-gather.5.cloned.1.call-update) | async-done | bytes 12582928 | tf_op jit(solution)/shard_map/all_gather | solution.py:82
  221.9 7.9 %fusion.1 = bf16[3072,128]{1,0:T(8,128)(2,1)} fusion(f32[3072,128]{1,0:T(8,128)} %fusion.27, bf16[3072,2048]{1,0:T(8,128)(2,1)} %all-gather.5.cloned.1.call-done, bf16[1,128,2048]{2,1,0:T(8,128)(2,1)S(1)} %copy-done.4), kind=kOutput, calls=%fused_computation.2 | convolution fusion | flops 1611399168 | bytes 15466496 | tf_op jit(solution)/shard_map/rh,dh->rd/dot_general | solution.py:57
  229.8 7.1 %all-to-all-start.1 = ((bf16[32,96,128]{2,1,0:T(8,128)(2,1)}), bf16[32,96,128]{2,1,0:T(8,128)(2,1)}, u32[]{:S(2)}, u32[]{:S(2)}) async-start(bf16[32,96,128]{2,1,0:T(8,128)(2,1)} %bitcast.14), calls=%async_computation.1 | async-start | bytes 1572864 | tf_op jit(solution)/shard_map/all_to_all | solution.py:86
  236.9 0.5 convolution_convert_fusion.2
  237.4 1.3 copy.47
  238.7 2.1 collective-permute-start
  241.8 1.2 copy.48
  243.0 16.9 %all-to-all-done.1 = bf16[32,96,128]{2,1,0:T(8,128)(2,1)} async-done(((bf16[32,96,128]{2,1,0:T(8,128)(2,1)}), bf16[32,96,128]{2,1,0:T(8,128)(2,1)}, u32[]{:S(2)}, u32[]{:S(2)}) %all-to-all-start.1) | async-done | bytes 786464 | tf_op jit(solution)/shard_map/all_to_all | solution.py:86
  259.9 5.4 %all-to-all-start = ((bf16[96,32,128]{2,0,1:T(8,128)(2,1)}), bf16[96,32,128]{2,0,1:T(8,128)(2,1)S(1)}, u32[]{:S(2)}, u32[]{:S(2)}) async-start(bf16[96,32,128]{2,0,1:T(8,128)(2,1)} %copy.48), calls=%async_computation | async-start | bytes 1572864 | tf_op jit(solution)/shard_map/all_to_all | solution.py:68
  265.3 16.5 %collective-permute-done = bf16[1,2,1,128,2048]{4,3,2,1,0:T(8,128)(2,1)} collective-permute-done((bf16[1,2,1,128,2048]{4,3,2,1,0:T(8,128)(2,1)}, bf16[1,2,1,128,2048]{4,3,2,1,0:T(8,128)(2,1)}, u32[]{:S(2)}, u32[]{:S(2)}) %collective-permute-start) | collective-permute-done | bytes 1048608 | tf_op jit(solution)/shard_map/ppermute | solution.py:15
  281.8 2.1 copy_bitcast_fusion
  283.9 15.3 %all-to-all-done = bf16[96,32,128]{2,0,1:T(8,128)(2,1)S(1)} async-done(((bf16[96,32,128]{2,0,1:T(8,128)(2,1)}), bf16[96,32,128]{2,0,1:T(8,128)(2,1)S(1)}, u32[]{:S(2)}, u32[]{:S(2)}) %all-to-all-start) | async-done | bytes 786464 | tf_op jit(solution)/shard_map/all_to_all | solution.py:68
  299.1 7.2 %fusion.2 = bf16[1,128,2048]{2,1,0:T(8,128)(2,1)} fusion(bf16[3072,128]{1,0:T(8,128)(2,1)S(1)} %bitcast.75, bf16[3072,2048]{1,0:T(8,128)(2,1)} %all-gather.3.cloned.1.call-done), kind=kOutput, calls=%fused_computation.5 | convolution fusion | flops 1610874880 | bytes 13893632 | tf_op jit(solution)/shard_map/rd,rh->dh/dot_general | solution.py:52
  306.4 7.2 %fusion.3 = bf16[1,128,2048]{2,1,0:T(8,128)(2,1)} fusion(bf16[3072,128]{1,0:T(8,128)(2,1)S(1)} %bitcast.76, bf16[3072,2048]{1,0:T(8,128)(2,1)} %all-gather.5.cloned.1.call-done), kind=kOutput, calls=%fused_computation.6 | convolution fusion | flops 1610874880 | bytes 13893632 | tf_op jit(solution)/shard_map/rd,rh->dh/dot_general | solution.py:53
  313.6 52.7 %all-reduce.2.cloned.1.call-done = bf16[96,4096]{1,0:T(8,128)(2,1)} async-done(((bf16[96,4096]{1,0:T(8,128)(2,1)}), bf16[96,4096]{1,0:T(8,128)(2,1)}) %all-reduce.2.cloned.1.call-update) | async-done | bytes 786448 | tf_op jit(solution)/shard_map/psum | solution.py:89
  366.3 1.7 fusion.11
  368.1 139.1 %psum.15 = f32[4096]{0:T(1024)} all-reduce(f32[4096]{0:T(1024)S(1)} %get-tuple-element.20), channel_id=1, replica_groups=mesh['section'=8,'dp'=32] {'dp'}, use_global_device_ids=true, to_apply=%region_7.0 | all-reduce | flops 4096 | bytes 32768 | tf_op jit(solution)/shard_map/psum | solution.py:95
  507.1 1.4 fusion.8
  508.5 2.3 copy.68
  (30 shorter events, 1.6 us)
Async XLA Ops:
  7.2 114.4 %copy-start = (bf16[1,128,2048]{2,1,0:T(8,128)(2,1)S(1)}, bf16[1,128,2048]{2,1,0:T(8,128)(2,1)}, u32[]{:S(2)}) copy-start(bf16[1,128,2048]{2,1,0:T(8,128)(2,1)} %param.14) | copy-start | bytes 1572868
  7.2 1.8 copy-start.5
  7.2 114.4 %all-gather.3.cloned.1.call-start = ((), (), s32[]{:S(2)}) async-start(), calls=%async_computation.2 | async-start | bytes 12976128 | tf_op jit(solution)/shard_map/all_gather | solution.py:81
  9.0 3.1 copy-start.6
  14.7 2.4 copy-start.3
  19.8 202.0 %all-gather.5.cloned.1.call-start = ((), (), s32[]{:S(2)}) async-start(), calls=%async_computation.3 | async-start | bytes 12976128 | tf_op jit(solution)/shard_map/all_gather | solution.py:82
  23.9 198.0 %copy-start.4 = (bf16[1,128,2048]{2,1,0:T(8,128)(2,1)S(1)}, bf16[1,128,2048]{2,1,0:T(8,128)(2,1)}, u32[]{:S(2)}) copy-start(bf16[1,128,2048]{2,1,0:T(8,128)(2,1)} %param.15) | copy-start | bytes 1572868
  229.8 30.1 %all-to-all-start.1 = ((bf16[32,96,128]{2,1,0:T(8,128)(2,1)}), bf16[32,96,128]{2,1,0:T(8,128)(2,1)}, u32[]{:S(2)}, u32[]{:S(2)}) async-start(bf16[32,96,128]{2,1,0:T(8,128)(2,1)} %bitcast.14), calls=%async_computation.1 | async-start | bytes 1572864 | tf_op jit(solution)/shard_map/all_to_all | solution.py:86
  237.4 3.4 copy-start.1
  238.7 43.0 %collective-permute-start = (bf16[1,2,1,128,2048]{4,3,2,1,0:T(8,128)(2,1)}, bf16[1,2,1,128,2048]{4,3,2,1,0:T(8,128)(2,1)}, u32[]{:S(2)}, u32[]{:S(2)}) collective-permute-start(bf16[1,2,1,128,2048]{4,3,2,1,0:T(8,128)(2,1)} %copy.47), channel_id=1, source_target_pairs={{32,0},{64,32},{96,64},{128,96},{160,128},{192,160},{224,192},{33,... | collective-permute-start | bytes 3145736 | tf_op jit(solution)/shard_map/ppermute | solution.py:15
  240.8 0.7 copy-start.7
  259.9 39.3 %all-to-all-start = ((bf16[96,32,128]{2,0,1:T(8,128)(2,1)}), bf16[96,32,128]{2,0,1:T(8,128)(2,1)S(1)}, u32[]{:S(2)}, u32[]{:S(2)}) async-start(bf16[96,32,128]{2,0,1:T(8,128)(2,1)} %copy.48), calls=%async_computation | async-start | bytes 1572864 | tf_op jit(solution)/shard_map/all_to_all | solution.py:68
  265.2 101.1 %all-reduce.2.cloned.1.call-start = ((), (), s32[]{:S(2)}) async-start(), calls=%async_computation.4 | async-start | bytes 1572864 | tf_op jit(solution)/shard_map/psum | solution.py:89
  366.3 140.8 %copy-start.2 = (bf16[96,4096]{1,0:T(8,128)(2,1)S(1)}, bf16[96,4096]{1,0:T(8,128)(2,1)}, u32[]{:S(2)}) copy-start(bf16[96,4096]{1,0:T(8,128)(2,1)} %all-reduce.2.cloned.1.call-done) | copy-start | bytes 2359300
Sparse Core Ops, SparseCore 0:
  20.0 101.5 all-gather.2
  124.7 97.1 all-gather.4
  284.0 82.2 all-reduce.1
where the time goes:
time: 518 us; the launch traced here: 517 us
  waiting for transfers between devices  292 us (56%)
  blocking collectives  139 us (27%)
  matrix products  37.9 us (7%)
  local copies, waits for them, and re-layouts  16.1 us (3%)
  starting transfers between devices  14.7 us (3%)
  between operations  13.9 us (3%)
    psum x1, blocking collectives, body(): gain_grad = lax.psum(jnp.sum(summed * hidden_f * inverse, axis=0), 'dp')  139 us
    all_gather x1, waiting for transfers between devices, body(): lax.all_gather(key_grad, 'dp', axis=0, tiled=True)  97.7 us
    all_gather x1, waiting for transfers between devices, body(): lax.all_gather(value_grad, 'dp', axis=0, tiled=True)  92.7 us
    psum x1, waiting for transfers between devices, body(): lax.psum(local_grad.astype(jnp.bfloat16), 'section').astype(jnp.float32)  52.7 us
    all_to_all x1, waiting for transfers between devices, body(): lax.all_to_all(returned.astype(jnp.bfloat16), 'dp', split_axis=0, concat_...  16.9 us
    ppermute x1, waiting for transfers between devices, from_behind(): lax.ppermute(value, axis, [(source, source + steps) for source in range(f...  16.5 us
    all_to_all x1, waiting for transfers between devices, body(): lax.all_to_all(memory, 'dp', split_axis=1, concat_axis=0, tiled=True)  15.3 us
  transfers between devices with their start and end apart: 6, of which 6 were waited for; matrix products, arithmetic and copies ran while one was open for 6% of the time, Pallas kernels for 0%

commit v1 on v0

v1 whole, which is shorter than its diff:
```python
import jax
import jax.numpy as jnp
from jax import lax
from jax.sharding import Mesh, PartitionSpec as P

HEAD_DIM = 64
EPS = 1e-06
BF = jnp.bfloat16
F32 = jnp.float32
SEC = ("y", "zlo")
ZC = ("zhi", "core")


def backward_heads(query_rows, key_rows, value_rows, grad_rows):
    batches, target_n, inner = query_rows.shape
    source_n = key_rows.shape[1]
    head_count = inner // HEAD_DIM
    query_h = query_rows.reshape(batches, target_n, head_count, HEAD_DIM)
    key_h = key_rows.reshape(batches, source_n, head_count, HEAD_DIM)
    value_h = value_rows.reshape(batches, source_n, head_count, HEAD_DIM)
    grad_h = grad_rows.reshape(batches, target_n, head_count, HEAD_DIM)
    scores = jnp.einsum("mshe,mthe->mhst", key_h, query_h, preferred_element_type=F32)
    highest = jnp.max(scores, axis=2, keepdims=True)
    exponent = jnp.exp(scores - highest)
    softmax_w = exponent / jnp.sum(exponent, axis=2, keepdims=True)
    rounded_w = softmax_w.astype(BF)
    slopes = jnp.einsum("mshe,mthe->mhst", value_h, grad_h, preferred_element_type=F32)
    center = jnp.sum(softmax_w * slopes, axis=2, keepdims=True)
    score_grad = (softmax_w * (slopes - center)).astype(BF)
    value_grad = jnp.einsum("mhst,mthe->mshe", rounded_w, grad_h, preferred_element_type=F32)
    key_grad = jnp.einsum("mhst,mthe->mshe", score_grad, query_h, preferred_element_type=F32)
    query_local = jnp.einsum("mhst,mshe->mthe", score_grad, key_h, preferred_element_type=F32)
    return (
        query_local.astype(BF).reshape(batches, target_n, inner),
        key_grad.astype(BF).reshape(batches * source_n, inner),
        value_grad.astype(BF).reshape(batches * source_n, inner),
    )


def body(pre_norm, norm_gain, queries, keys, values, head_grad, key_weight, value_weight):
    batches, _, source_n, features = pre_norm.shape
    rows = batches * source_n
    piece = rows // 8
    inner = queries.shape[-1]
    weights = lax.all_gather(
        jnp.stack([key_weight[0], value_weight[0]]), "x", axis=1, tiled=True
    )
    hidden = pre_norm.astype(F32).reshape(rows, features)
    inverse = lax.rsqrt(jnp.mean(hidden * hidden, axis=-1, keepdims=True) + EPS)
    memory = (hidden * inverse * norm_gain).astype(BF)
    split = memory.reshape(rows, 4, 4, 2, 128).transpose(1, 3, 0, 2, 4).reshape(8, rows, 512)
    columns = lax.all_to_all(split, ZC, split_axis=0, concat_axis=0, tiled=True)
    columns = columns.reshape(8 * rows, 512)

    query_local, key_grad, value_grad = backward_heads(
        queries[0, :, 0], keys[0, :, 0], values[0, :, 0], head_grad[0, :, 0]
    )
    value_all = lax.all_gather(value_grad, ZC, axis=0, tiled=True)
    key_all = lax.all_gather(key_grad, ZC, axis=0, tiled=True)
    returned = jnp.einsum("rh,dh->rd", value_all, weights[1], preferred_element_type=F32)
    returned += jnp.einsum("rh,dh->rd", key_all, weights[0], preferred_element_type=F32)
    gain_part = jnp.sum(returned * columns.astype(F32), axis=0)

    def shard(grad_all):
        partial = jnp.einsum("rd,rh->dh", columns, grad_all, preferred_element_type=F32)
        return lax.psum_scatter(partial.astype(BF), "x", scatter_dimension=0, tiled=True)

    grad_value = shard(value_all)
    grad_key = shard(key_all)

    returned = returned.astype(BF).reshape(8, 8, piece, 512).transpose(1, 0, 2, 3)
    layers = lax.all_to_all(returned, SEC, split_axis=0, concat_axis=0, tiled=True)
    summed = jnp.sum(layers.astype(F32), axis=0)
    gain_part = lax.psum(gain_part, "x")
    gain_hi = gain_part.astype(BF)
    gain_lo = (gain_part - gain_hi.astype(F32)).astype(BF)
    gain_rows = jnp.broadcast_to(jnp.stack([gain_hi, gain_lo])[None], (8, 2, 512))
    sent = jnp.concatenate([summed.astype(BF), gain_rows], axis=1)
    own = lax.all_to_all(sent, ZC, split_axis=0, concat_axis=0, tiled=True)
    own = own.reshape(4, 2, piece + 2, 4, 128).transpose(2, 0, 3, 1, 4).reshape(piece + 2, features)
    rank = lax.axis_index(SEC)
    my_hidden = lax.dynamic_slice_in_dim(hidden, rank * piece, piece, 0)
    my_inverse = lax.dynamic_slice_in_dim(inverse, rank * piece, piece, 0)
    scaled = norm_gain * own[:piece].astype(F32)
    row_mean = jnp.mean(my_hidden * scaled, axis=-1, keepdims=True)
    mine = my_inverse * scaled - my_hidden * my_inverse * my_inverse * my_inverse * row_mean
    packed = jnp.concatenate([mine.astype(BF), own[piece:]], axis=0)
    everyone = lax.all_to_all(
        jnp.broadcast_to(packed[None], (8,) + packed.shape), SEC, split_axis=0, concat_axis=0, tiled=True
    )
    encoder_grad = everyone[:, :piece].reshape(pre_norm.shape)
    gain_grad = jnp.sum(everyone[:, piece:].astype(F32), axis=(0, 1)) / norm_gain

    order = [(s, s - 1) for s in range(1, 8)]
    query_grad = lax.ppermute(query_local.reshape(queries.shape), SEC, order)
    return (query_grad, grad_key[None], grad_value[None], encoder_grad, gain_grad)


def solution(mesh):
    grid = Mesh(mesh.devices.reshape(4, 2, 4, 4, 2), ("y", "zlo", "zhi", "x", "core"))
    dp = ("zhi", "x", "core")
    return jax.shard_map(
        body,
        mesh=grid,
        in_specs=(
            P(None, dp, None, None),
            P(),
            P(SEC, None, dp, None, None),
            P(SEC, None, dp, None, None),
            P(SEC, None, dp, None, None),
            P(SEC, None, dp, None, None),
            P(SEC, dp, None),
            P(SEC, dp, None),
        ),
        out_specs=(
            P(SEC, None, dp, None, None),
            P(SEC, dp, None),
            P(SEC, dp, None),
            P(None, dp, None, None),
            P(),
        ),
        check_vma=False,
    )
```

time: 518 us -> 277 us (0.53)
  waiting for transfers between devices: 292 us -> 133 us
  blocking collectives: 139 us -> 59.9 us
  matrix products: 37.9 us -> 27.2 us
    psum x1, blocking collectives: 139 us -> 10.7 us  [body(): gain_part = lax.psum(gain_part, 'x')]
    all_gather x2 -> x3, waiting for transfers between devices: 190 us -> 94.2 us  [the longest x1 47.1 us: body(): lax.all_gather(jnp.stack([key_weight[0], value_weight[0]]), 'x', axis=1,...]
    psum x1 -> x0, waiting for transfers between devices: 52.7 us -> none  [body(): lax.psum(local_grad.astype(jnp.bfloat16), 'section').astype(jnp.float32)]
    all_to_all x0 -> x1, blocking collectives: none -> 49.2 us  [body(): columns = lax.all_to_all(split, ZC, split_axis=0, concat_axis=0, tiled=True)]
    all_to_all x2 -> x3, waiting for transfers between devices: 32.2 us -> 9.64 us  [the longest x1 9.64 us: body(): own = lax.all_to_all(sent, ZC, split_axis=0, concat_axis=0, tiled=True)]
    ppermute x1, waiting for transfers between devices: 16.5 us -> 29 us  [body(): query_grad = lax.ppermute(query_local.reshape(queries.shape), SEC, order)]
    dot_general x7, matrix products: 35.3 us -> 25.8 us  [the longest x2 10.1 us: shard(): jnp.einsum('rd,rh->dh', columns, grad_all, preferred_element_type=F32)]
    all_to_all x2 -> x3, starting transfers between devices: 12.5 us -> 14.4 us  [the longest x1 5.35 us: body(): lax.all_to_all(jnp.broadcast_to(packed[None], (8,) + packed.shape), SEC,...]
  transfers between devices with their start and end apart: 6 -> 9, of which waited for: 6 -> 5; matrix products, arithmetic and copies ran while one was open for 6% -> 14% of each run, Pallas kernels for 0% -> 0%
where the time goes in v1:
time: 277 us; the launch traced here: 276 us
  waiting for transfers between devices  133 us (48%)
  blocking collectives  59.9 us (22%)
  matrix products  27.2 us (10%)
  local copies, waits for them, and re-layouts  18.4 us (7%)
  starting transfers between devices  18 us (6%)
  between operations  14.1 us (5%)
  other arithmetic  6 us (2%)
    all_to_all x1, blocking collectives, body(): columns = lax.all_to_all(split, ZC, split_axis=0, concat_axis=0, tiled=True)  49.2 us
    all_gather x1, waiting for transfers between devices, body(): lax.all_gather(jnp.stack([key_weight[0], value_weight[0]]), 'x', axis=1,...  47.1 us
    all_gather x1, waiting for transfers between devices, body(): value_all = lax.all_gather(value_grad, ZC, axis=0, tiled=True)  41.6 us
    ppermute x1, waiting for transfers between devices, body(): query_grad = lax.ppermute(query_local.reshape(queries.shape), SEC, order)  29 us
    psum x1, blocking collectives, body(): gain_part = lax.psum(gain_part, 'x')  10.7 us
    dot_general x2, matrix products, shard(): jnp.einsum('rd,rh->dh', columns, grad_all, preferred_element_type=F32)  10.1 us
    all_to_all x1, waiting for transfers between devices, body(): own = lax.all_to_all(sent, ZC, split_axis=0, concat_axis=0, tiled=True)  9.64 us
    dot_general x1, matrix products, body(): jnp.einsum('rh,dh->rd', value_all, weights[1], preferred_element_type=F32)  5.71 us
  transfers between devices with their start and end apart: 9, of which 5 were waited for; matrix products, arithmetic and copies ran while one was open for 14% of the time, Pallas kernels for 0%

profile of v1, /device:TPU:8, one launch (start us, length us, event | category | flops | bytes accessed | tf_op | source)
XLA Modules:
  0.0 276.4 jit_solution(11272570022886157925)
XLA Ops:
  7.2 1.7 copy.44
  9.0 0.8 reshape_squeeze.12
  9.8 1.3 copy.46
  11.1 1.7 reshape_squeeze.14
  13.5 2.1 multiply_reduce_fusion.2
  16.9 1.4 reshape.100
  18.3 2.4 pad_maximum_fusion
  21.7 1.4 reshape.101
  23.2 1.6 reshape.97
  25.1 0.8 fusion.11
  26.4 49.2 %all_to_all.20 = bf16[8,96,512]{2,1,0:T(8,128)(2,1)S(1)} all-to-all(bf16[8,96,512]{2,1,0:T(8,128)(2,1)S(1)} %reshape.98), channel_id=1, replica_groups=mesh['y'=4,'zlo'=2,'zhi'=4,'x'=4,'core'=2] {'zhi','core'}, dimensions={0} | all-to-all | bytes 1572864 | tf_op jit(solution)/shard_map/all_to_all | solution.py:52
  75.7 5.5 %all-gather.4.cloned.1.call-done = bf16[768,2048]{1,0:T(8,128)(2,1)} async-done(((bf16[96,2048]{1,0:T(8,128)(2,1)}), bf16[768,2048]{1,0:T(8,128)(2,1)}) %all-gather.4.cloned.1.call-update) | async-done | bytes 3145744 | tf_op jit(solution)/shard_map/all_gather | solution.py:59
  81.1 5.0 %convolution_convert_fusion.1 = bf16[512,2048]{1,0:T(8,128)(2,1)} fusion(bf16[768,512]{1,0:T(8,128)(2,1)S(1)} %bitcast.57, bf16[768,2048]{1,0:T(8,128)(2,1)} %all-gather.4.cloned.1.call-done), kind=kOutput, calls=%fused_computation.2 | convolution fusion | flops 1611661312 | bytes 6029312 | tf_op jit(solution)/shard_map/rd,rh->dh/dot_general | solution.py:65
  86.2 47.1 %all-gather.8.cloned.1.call-done = bf16[2,512,2048]{2,1,0:T(8,128)(2,1)} async-done(((bf16[2,128,2048]{2,1,0:T(8,128)(2,1)}), bf16[2,512,2048]{2,1,0:T(8,128)(2,1)}) %all-gather.8.cloned.1.call-update) | async-done | bytes 4194320 | tf_op jit(solution)/shard_map/all_gather | solution.py:45
  133.3 5.6 %fusion.1 = f32[768,512]{1,0:T(8,128)} fusion(bf16[768,2048]{1,0:T(8,128)(2,1)} %all-gather.4.cloned.1.call-done, bf16[2,512,2048]{2,1,0:T(8,128)(2,1)} %all-gather.8.cloned.1.call-done), kind=kOutput, calls=%fused_computation.4 | convolution fusion | flops 1610612736 | bytes 6815744 | tf_op jit(solution)/shard_map/rh,dh->rd/dot_general | solution.py:61
  138.8 41.6 %all-gather.6.cloned.1.call-done = bf16[768,2048]{1,0:T(8,128)(2,1)} async-done(((bf16[96,2048]{1,0:T(8,128)(2,1)}), bf16[768,2048]{1,0:T(8,128)(2,1)}) %all-gather.6.cloned.1.call-update) | async-done | bytes 3145744 | tf_op jit(solution)/shard_map/all_gather | solution.py:58
  180.4 5.7 %fusion.15 = (bf16[768,512]{1,0:T(8,128)(2,1)}, f32[512]{0:T(512)S(1)}) fusion(bf16[8,96,512]{2,1,0:T(8,128)(2,1)S(1)} %all_to_all.20, f32[768,512]{1,0:T(8,128)} %fusion.1, bf16[768,2048]{1,0:T(8,128)(2,1)} %all-gather.6.cloned.1.call-done, bf16[2,512,2048]{2,1,0:T(8,128)(2,1)} %all-gather.8.cloned.1.call-done), kind=kOutput, calls=%fused_computation.41 | convolution fusion | flops 1612578304 | bytes 8390656 | tf_op jit(solution)/shard_map/rh,dh->rd/dot_general | solution.py:60
  186.2 1.2 reshape.102
  187.4 1.3 copy.53
  188.7 4.8 %all-to-all-start.1 = ((bf16[8,8,12,512]{3,1,2,0:T(8,128)(2,1)}), bf16[8,8,12,512]{3,1,2,0:T(8,128)(2,1)S(1)}, u32[]{:S(2)}, u32[]{:S(2)}) async-start(bf16[8,8,12,512]{3,1,2,0:T(8,128)(2,1)} %copy.53), calls=%async_computation.3 | async-start | bytes 1572864 | tf_op jit(solution)/shard_map/all_to_all | solution.py:72
  193.6 5.1 %convolution_convert_fusion = bf16[512,2048]{1,0:T(8,128)(2,1)} fusion(bf16[768,512]{1,0:T(8,128)(2,1)S(1)} %bitcast.58, bf16[768,2048]{1,0:T(8,128)(2,1)} %all-gather.6.cloned.1.call-done), kind=kOutput, calls=%fused_computation.1 | convolution fusion | flops 1611661312 | bytes 6029312 | tf_op jit(solution)/shard_map/rd,rh->dh/dot_general | solution.py:65
  198.7 10.7 %psum.7 = f32[512]{0:T(512)S(1)} all-reduce(f32[512]{0:T(512)S(1)} %get-tuple-element.23), channel_id=1, replica_groups=mesh['y'=4,'zlo'=2,'zhi'=4,'x'=4,'core'=2] {'x'}, use_global_device_ids=true, to_apply=%region_8.0 | all-reduce | flops 512 | bytes 4096 | tf_op jit(solution)/shard_map/psum | solution.py:74
  210.3 4.3 %all-to-all-start.2 = ((bf16[8,14,512]{2,1,0:T(8,128)(2,1)}), bf16[8,14,512]{2,1,0:T(8,128)(2,1)S(1)}, u32[]{:S(2)}, u32[]{:S(2)}) async-start(bf16[8,14,512]{2,1,0:T(8,128)(2,1)} %pad_maximum_fusion.1), calls=%async_computation.4 | async-start | bytes 262144 | tf_op jit(solution)/shard_map/all_to_all | solution.py:79
  214.9 9.6 %all-to-all-done.2 = bf16[8,14,512]{2,1,0:T(8,128)(2,1)S(1)} async-done(((bf16[8,14,512]{2,1,0:T(8,128)(2,1)}), bf16[8,14,512]{2,1,0:T(8,128)(2,1)S(1)}, u32[]{:S(2)}, u32[]{:S(2)}) %all-to-all-start.2) | async-done | bytes 114720 | tf_op jit(solution)/shard_map/all_to_all | solution.py:79
  225.3 1.1 broadcast_in_dim.11
  226.4 5.3 %all-to-all-start.3 = ((bf16[8,14,4096]{2,1,0:T(8,128)(2,1)}), bf16[8,14,4096]{2,1,0:T(8,128)(2,1)S(1)}, u32[]{:S(2)}, u32[]{:S(2)}) async-start(bf16[8,14,4096]{2,1,0:T(8,128)(2,1)} %broadcast_in_dim.11), calls=%async_computation.5 | async-start | bytes 2097152 | tf_op jit(solution)/shard_map/all_to_all | solution.py:88
  231.7 1.6 convolution_convert_fusion.2
  233.4 1.3 copy.49
  234.7 3.4 %collective-permute-start = (bf16[1,2,1,128,2048]{4,3,2,1,0:T(8,128)(2,1)}, bf16[1,2,1,128,2048]{4,3,2,1,0:T(8,128)(2,1)S(1)}, u32[]{:S(2)}, u32[]{:S(2)}) collective-permute-start(bf16[1,2,1,128,2048]{4,3,2,1,0:T(8,128)(2,1)} %copy.49), channel_id=1, source_target_pairs={{32,0},{64,32},{96,64},{128,96},{160,128},{192,160},{224,192},{33,... | collective-permute-start | bytes 3145736 | tf_op jit(solution)/shard_map/ppermute | solution.py:95
  238.1 29.0 %collective-permute-done = bf16[1,2,1,128,2048]{4,3,2,1,0:T(8,128)(2,1)S(1)} collective-permute-done((bf16[1,2,1,128,2048]{4,3,2,1,0:T(8,128)(2,1)}, bf16[1,2,1,128,2048]{4,3,2,1,0:T(8,128)(2,1)S(1)}, u32[]{:S(2)}, u32[]{:S(2)}) %collective-permute-start) | collective-permute-done | bytes 1048608 | tf_op jit(solution)/shard_map/ppermute | solution.py:95
  267.1 1.1 reshape.105
  268.9 1.0 copy.74
  (64 shorter events, 6.8 us)
Async XLA Ops:
  7.2 1.8 copy-start.4
  7.2 2.6 copy-start.2
  7.2 73.9 %all-gather.4.cloned.1.call-start = ((), (), s32[]{:S(2)}) async-start(), calls=%async_computation.6 | async-start | bytes 3538944 | tf_op jit(solution)/shard_map/all_gather | solution.py:59
  9.8 3.0 %copy-start.1 = (bf16[2,48,32,64]{3,2,1,0:T(8,128)(2,1)}, bf16[2,48,32,64]{3,2,1,0:T(8,128)(2,1)S(1)}, u32[]{:S(2)}) copy-start(bf16[2,48,32,64]{3,2,1,0:T(8,128)(2,1)S(1)} %reshape_squeeze.12) | copy-start | bytes 1179652
  9.8 1.3 copy-start.5
  18.3 2.5 copy-start.3
  18.3 115.0 %all-gather.8.cloned.1.call-start = ((), (), s32[]{:S(2)}) async-start(), calls=%async_computation.10 | async-start | bytes 5242880 | tf_op jit(solution)/shard_map/all_gather | solution.py:45
  20.8 159.7 %all-gather.6.cloned.1.call-start = ((), (), s32[]{:S(2)}) async-start(), calls=%async_computation.8 | async-start | bytes 3538944 | tf_op jit(solution)/shard_map/all_gather | solution.py:58
  21.5 1.7 copy-start
  23.1 2.0 copy-start.6
  23.1 245.8 %reduce-scatter.3.cloned.1.call-start = ((), (), s32[]{:S(2)}) async-start(), calls=%async_computation.7 | async-start | bytes 2621440 | tf_op jit(solution)/shard_map/reduce_scatter | solution.py:66
  188.7 20.7 %all-to-all-start.1 = ((bf16[8,8,12,512]{3,1,2,0:T(8,128)(2,1)}), bf16[8,8,12,512]{3,1,2,0:T(8,128)(2,1)S(1)}, u32[]{:S(2)}, u32[]{:S(2)}) async-start(bf16[8,8,12,512]{3,1,2,0:T(8,128)(2,1)} %copy.53), calls=%async_computation.3 | async-start | bytes 1572864 | tf_op jit(solution)/shard_map/all_to_all | solution.py:72
  193.6 75.4 %reduce-scatter.5.cloned.1.call-start = ((), (), s32[]{:S(2)}) async-start(), calls=%async_computation.9 | async-start | bytes 2621440 | tf_op jit(solution)/shard_map/reduce_scatter | solution.py:66
  210.3 14.2 %all-to-all-start.2 = ((bf16[8,14,512]{2,1,0:T(8,128)(2,1)}), bf16[8,14,512]{2,1,0:T(8,128)(2,1)S(1)}, u32[]{:S(2)}, u32[]{:S(2)}) async-start(bf16[8,14,512]{2,1,0:T(8,128)(2,1)} %pad_maximum_fusion.1), calls=%async_computation.4 | async-start | bytes 262144 | tf_op jit(solution)/shard_map/all_to_all | solution.py:79
  226.4 40.7 %all-to-all-start.3 = ((bf16[8,14,4096]{2,1,0:T(8,128)(2,1)}), bf16[8,14,4096]{2,1,0:T(8,128)(2,1)S(1)}, u32[]{:S(2)}, u32[]{:S(2)}) async-start(bf16[8,14,4096]{2,1,0:T(8,128)(2,1)} %broadcast_in_dim.11), calls=%async_computation.5 | async-start | bytes 2097152 | tf_op jit(solution)/shard_map/all_to_all | solution.py:88
  234.7 32.4 %collective-permute-start = (bf16[1,2,1,128,2048]{4,3,2,1,0:T(8,128)(2,1)}, bf16[1,2,1,128,2048]{4,3,2,1,0:T(8,128)(2,1)S(1)}, u32[]{:S(2)}, u32[]{:S(2)}) collective-permute-start(bf16[1,2,1,128,2048]{4,3,2,1,0:T(8,128)(2,1)} %copy.49), channel_id=1, source_target_pairs={{32,0},{64,32},{96,64},{128,96},{160,128},{192,160},{224,192},{33,... | collective-permute-start | bytes 3145736 | tf_op jit(solution)/shard_map/ppermute | solution.py:95
Sparse Core Ops, SparseCore 0:
  18.4 62.6 all-gather.3
  82.9 50.2 all-gather.7
  135.7 44.7 all-gather.5
  183.4 30.5 reduce-scatter.2
  217.2 31.8 reduce-scatter.4

commit v2 on v1

v2 whole, which is shorter than its diff:
```python
import functools

import jax
import jax.numpy as jnp
from jax import lax
from jax.experimental import pallas as pl
from jax.experimental.pallas import tpu as pltpu
from jax.sharding import Mesh, PartitionSpec as P

EPS = 1e-06
BF = jnp.bfloat16
F32 = jnp.float32
SEC = ("y", "zlo")
ZC = ("zhi", "core")
SRC = 48
D = 4096
HD = 2048
COLS = 512
PIECE = 6
VMEM = pl.BlockSpec(memory_space=pltpu.VMEM)
HBM = pl.BlockSpec(memory_space=pl.ANY)
SMEM = pl.BlockSpec(memory_space=pltpu.SMEM)


def shape(dims, dtype=BF):
    return jax.ShapeDtypeStruct(dims, dtype)


def params(mib=32):
    return pltpu.CompilerParams(vmem_limit_bytes=mib * 2**20)


def cost(flops, size):
    return pl.CostEstimate(flops=flops, bytes_accessed=size, transcendentals=0)


def rows_dot(a, b):
    return lax.dot_general(a, b, (((1,), (1,)), ((), ())), preferred_element_type=F32)


def columns_dot(a, b):
    return lax.dot_general(a, b, (((0,), (0,)), ((), ())), preferred_element_type=F32)


def heads_kernel(q_ref, k_ref, v_ref, g_ref, local_ref, grads_ref):
    src = k_ref.shape[0]
    lane = lax.broadcasted_iota(jnp.int32, (src, 256), 1) // 64
    masks = [lane == h for h in range(4)]

    def spread(block):
        zero = jnp.zeros_like(block)
        return jnp.concatenate([jnp.where(m, block, zero) for m in masks], axis=0)

    def diagonal(wide):
        out = wide[:src]
        for h in range(1, 4):
            out = jnp.where(masks[h], wide[h * src : (h + 1) * src], out)
        return out

    for part in range(HD // 256):
        at = pl.ds(part * 256, 256)
        q, g = q_ref[:, at], g_ref[:, at]
        k, v = spread(k_ref[:, at]), spread(v_ref[:, at])
        scores = rows_dot(k, q).reshape(4, src, -1)
        exponent = jnp.exp(scores - jnp.max(scores, axis=1, keepdims=True))
        probs = exponent * (1.0 / jnp.sum(exponent, axis=1, keepdims=True))
        slopes = rows_dot(v, g).reshape(4, src, -1)
        center = jnp.sum(probs * slopes, axis=1, keepdims=True)
        score_grad = (probs * (slopes - center)).astype(BF).reshape(4 * src, -1)
        probs = probs.astype(BF).reshape(4 * src, -1)
        value = jnp.dot(probs, g, preferred_element_type=F32)
        key = jnp.dot(score_grad, q, preferred_element_type=F32)
        grads_ref[:, at] = diagonal(key).astype(BF)
        grads_ref[:, pl.ds(HD + part * 256, 256)] = diagonal(value).astype(BF)
        local_ref[:, at] = columns_dot(score_grad, k).astype(BF)


def heads(q, k, v, g, m):
    tgt = q.shape[3]

    def row(n):
        return pl.BlockSpec((None, None, None, n, HD), lambda i: (0, m, 0, 0, 0))

    return pl.pallas_call(
        heads_kernel,
        grid=(1,),
        in_specs=[row(tgt), row(SRC), row(SRC), row(tgt)],
        out_specs=[pl.BlockSpec((tgt, HD), lambda i: (0, 0)), pl.BlockSpec((SRC, D), lambda i: (0, 0))],
        out_shape=[shape((tgt, HD)), shape((SRC, D))],
        compiler_params=params(),
        cost_estimate=cost(2 * 10**9, 3 * 10**6),
        name="heads",
    )(q, k, v, g)


def memory_kernel(pre_ref, gain_ref, out_ref):
    hidden = pre_ref[...].astype(F32)
    inverse = lax.rsqrt(jnp.mean(hidden * hidden, axis=-1, keepdims=True) + EPS)
    memory = (hidden * inverse * gain_ref[...]).astype(BF)
    for z in range(4):
        for c in range(2):
            for x in range(4):
                start = ((z * 4 + x) * 2 + c) * 128
                out_ref[z * 2 + c, :, x * 128 : (x + 1) * 128] = memory[:, start : start + 128]


def memory_blocks(pre, gain):
    rows = pre.shape[0]
    return pl.pallas_call(
        memory_kernel,
        in_specs=[VMEM, VMEM],
        out_specs=VMEM,
        out_shape=shape((8, rows, COLS)),
        compiler_params=params(),
        cost_estimate=cost(4 * 10**6, 2 * 10**6),
        name="memory",
    )(pre, gain)


def token_blocks(place_ref):
    z, c = place_ref[0], place_ref[1]
    index = []
    for core in (c, 1 - c):
        for step in (0, 3, 1, 2):
            index.append(lax.rem(z + step, 4) * 2 + core)
    return index


def return_kernel(m, place_ref, *refs):
    grads, keys, values = refs[:8], refs[8:12], refs[12:16]
    cols_ref, out_ref, gain_ref, grad_s, weight_s, cols_s, acc_s, sems = refs[16:]
    x = place_ref[2]
    copies = []
    for r in range(4):
        at = lax.rem(x + r, 4)
        copies.append((keys[r], weight_s.at[at, :, pl.ds(0, HD)]))
        copies.append((values[r], weight_s.at[at, :, pl.ds(HD, HD)]))
    for ref, zc in zip(grads, token_blocks(place_ref)):
        copies.append((ref, grad_s.at[zc]))
    copies.append((cols_ref.at[:, m], cols_s))
    copies = [pltpu.make_async_copy(a, b, sems.at[i]) for i, (a, b) in enumerate(copies)]
    for copy in copies:
        copy.start()
    for copy in copies:
        copy.wait()
    grad = grad_s[...].reshape(8 * SRC, D)
    for n in range(2):
        weight = weight_s[pl.ds(2 * n, 2)].reshape(256, D)
        acc_s[:, pl.ds(256 * n, 256)] = rows_dot(grad, weight)
    result = acc_s[...]
    columns = cols_s[...].reshape(8 * SRC, COLS).astype(F32)
    gain = jnp.sum(result * columns, axis=0, keepdims=True)
    gain_ref[...] = jnp.broadcast_to(gain, gain_ref.shape)
    rows = 8 * SRC
    target = lax.broadcasted_iota(jnp.int32, (rows, rows), 0)
    source = lax.broadcasted_iota(jnp.int32, (rows, rows), 1)
    rank, rest = target // SRC, target % SRC
    wanted = (rest // PIECE) * SRC + rank * PIECE + rest % PIECE
    move = (source == wanted).astype(F32).astype(BF)
    moved = jnp.dot(move, result.astype(BF), preferred_element_type=F32)
    out_ref[...] = moved.astype(BF).reshape(8, SRC, COLS)


def return_blocks(m, place, grads, keys, values, columns):
    return pl.pallas_call(
        functools.partial(return_kernel, m),
        in_specs=[SMEM] + [HBM] * 17,
        out_specs=[VMEM, VMEM],
        out_shape=[shape((8, SRC, COLS)), shape((8, COLS), F32)],
        scratch_shapes=[
            pltpu.VMEM((8, SRC, D), BF),
            pltpu.VMEM((4, 128, D), BF),
            pltpu.VMEM((8, SRC, COLS), BF),
            pltpu.VMEM((8 * SRC, COLS), F32),
            pltpu.SemaphoreType.DMA((17,)),
        ],
        compiler_params=params(),
        cost_estimate=cost(2 * 384 * 4096 * 512, 8 * 10**6),
        name="returned",
    )(place, *grads, *keys, *values, columns)


def weight_kernel(place_ref, *refs):
    grads, cols_ref, outs = refs[:16], refs[16], refs[17:25]
    grad_s, cols_s, sems = refs[25:]
    x = place_ref[2]
    copies = []
    for r in range(4):
        at = pl.ds(pl.multiple_of(lax.rem(x + r, 4) * 128, 128), 128)
        for m in range(2):
            copies.append((cols_ref.at[:, m, :, at], cols_s.at[m, :, :, pl.ds(r * 128, 128)]))
    blocks = token_blocks(place_ref)
    for m in range(2):
        for i, zc in enumerate(blocks):
            copies.append((grads[8 * m + i], grad_s.at[m, zc]))
    copies = [pltpu.make_async_copy(a, b, sems.at[i]) for i, (a, b) in enumerate(copies)]
    for copy in copies:
        copy.start()
    for copy in copies:
        copy.wait()
    columns = cols_s[...].reshape(16 * SRC, COLS)
    for half in range(2):
        for n in range(HD // 512):
            grad = grad_s[:, :, :, pl.ds(half * HD + n * 512, 512)].reshape(16 * SRC, 512)
            partial = columns_dot(columns, grad).astype(BF)
            for r in range(4):
                outs[half * 4 + r][:, pl.ds(n * 512, 512)] = partial[r * 128 : (r + 1) * 128]


def weight_blocks(place, grads, columns):
    return pl.pallas_call(
        weight_kernel,
        in_specs=[SMEM] + [HBM] * 17,
        out_specs=[VMEM] * 8,
        out_shape=[shape((128, HD))] * 8,
        scratch_shapes=[
            pltpu.VMEM((2, 8, SRC, D), BF),
            pltpu.VMEM((2, 8, SRC, COLS), BF),
            pltpu.SemaphoreType.DMA((24,)),
        ],
        compiler_params=params(),
        cost_estimate=cost(2 * 768 * 4096 * 512, 11 * 10**6),
        name="weights",
    )(place, *grads, columns)


def sum_kernel(layers_ref, gains_ref, out_ref):
    total = jnp.sum(layers_ref[...].astype(F32), axis=0).astype(BF)
    target = lax.broadcasted_iota(jnp.int32, (64, SRC), 0)
    source = lax.broadcasted_iota(jnp.int32, (64, SRC), 1)
    wanted = (target // 8) * PIECE + target % 8
    move = ((source == wanted) & (target % 8 < PIECE)).astype(F32).astype(BF)
    moved = jnp.dot(move, total, preferred_element_type=F32)
    gain = jnp.sum(gains_ref[...], axis=0, keepdims=True)
    high = gain.astype(BF).astype(F32)
    row = lax.broadcasted_iota(jnp.int32, (64, COLS), 0) % 8
    moved = jnp.where(row == 6, high, jnp.where(row == 7, gain - high, moved))
    out_ref[...] = moved.astype(BF).reshape(8, 8, COLS)


def sum_layers(layers, gains):
    return pl.pallas_call(
        sum_kernel,
        in_specs=[VMEM, VMEM],
        out_specs=VMEM,
        out_shape=shape((8, 8, COLS)),
        compiler_params=params(),
        cost_estimate=cost(4 * 10**6, 10**6),
        name="layers",
    )(layers, gains)


def encoder_kernel(place_ref, own_ref, pre_ref, gain_ref, out_ref, full_s):
    for z in range(4):
        for c in range(2):
            for x in range(4):
                start = ((z * 4 + x) * 2 + c) * 128
                full_s[:, start : start + 128] = own_ref[z * 2 + c, :, x * 128 : (x + 1) * 128]
    own = full_s[...].astype(F32)
    target = lax.broadcasted_iota(jnp.int32, (8, SRC), 0)
    source = lax.broadcasted_iota(jnp.int32, (8, SRC), 1)
    pick = ((source == place_ref[3] * PIECE + target) & (target < PIECE)).astype(F32).astype(BF)
    hidden = jnp.dot(pick, pre_ref[...], preferred_element_type=F32)
    inverse = lax.rsqrt(jnp.mean(hidden * hidden, axis=-1, keepdims=True) + EPS)
    scaled = own * gain_ref[...]
    row_mean = jnp.mean(hidden * scaled, axis=-1, keepdims=True)
    mine = inverse * scaled - hidden * (inverse * inverse * inverse * row_mean)
    row = lax.broadcasted_iota(jnp.int32, (8, D), 0)
    packed = jnp.where(row < PIECE, mine, own).astype(BF)
    for s in range(8):
        out_ref[s] = packed


def encoder_rows(place, own, pre, gain, m):
    return pl.pallas_call(
        encoder_kernel,
        grid=(1,),
        in_specs=[
            SMEM,
            pl.BlockSpec((8, 8, COLS), lambda i: (0, 0, 0)),
            pl.BlockSpec((None, None, SRC, D), lambda i: (m, 0, 0, 0)),
            pl.BlockSpec((1, D), lambda i: (0, 0)),
        ],
        out_specs=pl.BlockSpec((8, 8, D), lambda i: (0, 0, 0)),
        out_shape=shape((8, 8, D)),
        scratch_shapes=[pltpu.VMEM((8, D), BF)],
        compiler_params=params(),
        cost_estimate=cost(10**6, 10**6),
        name="encoder",
    )(place, own, pre, gain)


def finish_kernel(first_ref, second_ref, gain_ref, out_ref, gain_out_ref):
    target = lax.broadcasted_iota(jnp.int32, (SRC, 64), 0)
    source = lax.broadcasted_iota(jnp.int32, (SRC, 64), 1)
    wanted = (target // PIECE) * 8 + target % PIECE
    move = (source == wanted).astype(F32).astype(BF)
    for m, ref in enumerate((first_ref, second_ref)):
        packed = ref[...].reshape(64, D)
        out_ref[m, 0] = jnp.dot(move, packed, preferred_element_type=F32).astype(BF)
    row = lax.broadcasted_iota(jnp.int32, (64, D), 0) % 8
    terms = jnp.where(row >= PIECE, second_ref[...].reshape(64, D).astype(F32), 0.0)
    gain_out_ref[...] = jnp.sum(terms, axis=0, keepdims=True) / gain_ref[...]


def finish(first, second, gain):
    return pl.pallas_call(
        finish_kernel,
        in_specs=[VMEM] * 3,
        out_specs=[VMEM, VMEM],
        out_shape=[shape((2, 1, SRC, D)), shape((1, D), F32)],
        compiler_params=params(),
        cost_estimate=cost(10**6, 2 * 10**6),
        name="finish",
    )(first, second, gain)


def shift(value, axis, step):
    return lax.ppermute(value, axis, [(i, (i + step) % 4) for i in range(4)])


def swap(value):
    return lax.ppermute(value, "core", [(0, 1), (1, 0)])


def after(value, *others):
    return lax.optimization_barrier((value,) + others)[0]


def exchange(value, axes):
    return lax.all_to_all(value, axes, split_axis=0, concat_axis=0, tiled=True)


def body(pre_norm, norm_gain, queries, keys, values, head_grad, key_weight, value_weight):
    batches, _, source_n, features = pre_norm.shape
    place = jnp.stack(
        [lax.axis_index("zhi"), lax.axis_index("core"), lax.axis_index("x"), lax.axis_index(SEC)]
    ).astype(jnp.int32)
    gain = norm_gain.reshape(1, features)
    key_w, value_w = key_weight[0], value_weight[0]

    key_m, key_p = shift(key_w, "x", 1), shift(key_w, "x", -1)
    value_m, value_p = shift(value_w, "x", 1), shift(value_w, "x", -1)
    key_2, value_2 = shift(key_m, "x", 1), shift(value_p, "x", -1)
    keys_all = (key_w, key_p, key_2, key_m)
    values_all = (value_w, value_p, value_2, value_m)

    blocks = memory_blocks(pre_norm.reshape(batches * source_n, features), gain)
    columns = exchange(blocks, ZC).reshape(8, batches, source_n, COLS)

    local0, own0 = heads(queries, keys, values, head_grad, 0)
    minus0, plus0 = shift(own0, "zhi", 1), shift(own0, "zhi", -1)
    local1, own1 = heads(queries, keys, values, head_grad, 1)
    far0 = shift(minus0, "zhi", 1)
    plus1 = shift(after(own1, plus0), "zhi", -1)
    minus1 = shift(after(own1, far0), "zhi", 1)
    far1 = shift(plus1, "zhi", -1)
    grads0 = [own0, minus0, plus0, far0]
    grads0 += [swap(v) for v in grads0]
    grads1 = [own1, minus1, plus1, far1]
    grads1 += [swap(v) for v in grads1]

    def encoder(m, returned, gains):
        layers = exchange(returned, SEC)
        own = exchange(sum_layers(layers, gains), ZC)
        return exchange(encoder_rows(place, own, pre_norm, gain, m), SEC)

    returned0, gain0 = return_blocks(0, place, grads0, keys_all, values_all, columns)
    first = encoder(0, returned0, jnp.zeros((4, COLS), F32))
    returned1, gain1 = return_blocks(1, place, grads1, keys_all, values_all, columns)
    gain_part = gain0 + gain1
    gains = jnp.stack([gain_part[0]] + [shift(gain_part, "x", i)[0] for i in (1, 2, 3)])
    second = encoder(1, returned1, gains)

    partial = weight_blocks(place, grads0 + grads1, columns)
    key_part, value_part = partial[:4], partial[4:]

    def add(*terms):
        return sum(t.astype(F32) for t in terms).astype(BF)

    key_far, value_far = shift(key_part[2], "x", 1), shift(value_part[2], "x", -1)
    key_back, value_on = shift(key_part[3], "x", -1), shift(value_part[1], "x", 1)
    key_on = shift(add(key_part[1], key_far), "x", 1)
    value_back = shift(add(value_part[3], value_far), "x", -1)
    grad_key = add(key_part[0], key_on, key_back)
    grad_value = add(value_part[0], value_on, value_back)

    query_local = jnp.stack([local0, local1]).reshape(queries.shape)
    query_grad = lax.ppermute(query_local, SEC, [(s, s - 1) for s in range(1, 8)])
    encoder_grad, gain_grad = finish(first, second, gain)
    return (
        query_grad,
        grad_key[None],
        grad_value[None],
        encoder_grad,
        gain_grad.reshape(features),
    )


def solution(mesh):
    grid = Mesh(mesh.devices.reshape(4, 2, 4, 4, 2), ("y", "zlo", "zhi", "x", "core"))
    dp = ("zhi", "x", "core")
    return jax.shard_map(
        body,
        mesh=grid,
        in_specs=(
            P(None, dp, None, None),
            P(),
            P(SEC, None, dp, None, None),
            P(SEC, None, dp, None, None),
            P(SEC, None, dp, None, None),
            P(SEC, None, dp, None, None),
            P(SEC, dp, None),
            P(SEC, dp, None),
        ),
        out_specs=(
            P(SEC, None, dp, None, None),
            P(SEC, dp, None),
            P(SEC, dp, None),
            P(None, dp, None, None),
            P(),
        ),
        check_vma=False,
    )
```

time: 277 us -> 229 us (0.83)
  waiting for transfers between devices: 133 us -> 58.2 us
  starting transfers between devices: 18 us -> 91.5 us
  blocking collectives: 59.9 us -> 0 us
  Pallas kernels: 0 us -> 31 us
  matrix products: 27.2 us -> 0 us
  local copies, waits for them, and re-layouts: 18.4 us -> 34.9 us
  between operations: 14.1 us -> 0.94 us
  other arithmetic: 6 us -> 9.47 us
    all_gather x3 -> x0, waiting for transfers between devices: 94.2 us -> none  [the longest x1 47.1 us: body(): lax.all_gather(jnp.stack([key_weight[0], value_weight[0]]), 'x', axis=1,...]
    all_to_all x1 -> x0, blocking collectives: 49.2 us -> none  [body(): columns = lax.all_to_all(split, ZC, split_axis=0, concat_axis=0, tiled=True)]
    ppermute x1 -> x30, starting transfers between devices: 3.36 us -> 52.5 us  [the longest x21 48.2 us: shift(): return lax.ppermute(value, axis, [(i, (i + step) % 4) for i in range(4)])]
    pallas_call x0 -> x11, Pallas kernels: none -> 31 us  [the longest x2 10.5 us: return_blocks(): pl.pallas_call(functools.partial(return_kernel, m), in_specs=[SMEM] + [HB...]
    unnamed x18 -> x103, local copies, waits for them, and re-layouts: 4.07 us -> 34.9 us
    dot_general x8 -> x0, matrix products: 26.5 us -> none  [the longest x2 10.1 us: shard(): jnp.einsum('rd,rh->dh', columns, grad_all, preferred_element_type=F32)]
    all_to_all x3 -> x7, starting transfers between devices: 14.4 us -> 39 us  [exchange(): return lax.all_to_all(value, axes, split_axis=0, concat_axis=0, tiled=True)]
    ppermute x1 -> x30, waiting for transfers between devices: 29 us -> 46.5 us  [the longest x21 38.4 us: shift(): return lax.ppermute(value, axis, [(i, (i + step) % 4) for i in range(4)])]
  transfers between devices with their start and end apart: 9 -> 37, of which waited for: 5 -> 15; matrix products, arithmetic and copies ran while one was open for 14% -> 4% of each run, Pallas kernels for 0% -> 12%
where the time goes in v2:
time: 229 us; the launch traced here: 226 us
  starting transfers between devices  91.5 us (40%)
  waiting for transfers between devices  58.2 us (25%)
  local copies, waits for them, and re-layouts  34.9 us (15%)
  Pallas kernels  31 us (14%)
  other arithmetic  9.47 us (4%)
    ppermute x21, starting transfers between devices, shift(): return lax.ppermute(value, axis, [(i, (i + step) % 4) for i in range(4)])  48.2 us
    all_to_all x7, starting transfers between devices, exchange(): return lax.all_to_all(value, axes, split_axis=0, concat_axis=0, tiled=True)  39 us
    ppermute x21, waiting for transfers between devices, shift(): return lax.ppermute(value, axis, [(i, (i + step) % 4) for i in range(4)])  38.4 us
    unnamed x103, local copies, waits for them, and re-layouts  34.9 us
    all_to_all x7, waiting for transfers between devices, exchange(): return lax.all_to_all(value, axes, split_axis=0, concat_axis=0, tiled=True)  11.6 us
    pallas_call x2, Pallas kernels, return_blocks(): pl.pallas_call(functools.partial(return_kernel, m), in_specs=[SMEM] + [HB...  10.5 us
    pallas_call x1, Pallas kernels, weight_blocks(): pl.pallas_call(weight_kernel, in_specs=[SMEM] + [HBM] * 17, out_specs=[VM...  7.5 us
    ppermute x1, waiting for transfers between devices, body(): lax.ppermute(query_local, SEC, [(s, s - 1) for s in range(1, 8)])  5.5 us
  transfers between devices with their start and end apart: 37, of which 15 were waited for; matrix products, arithmetic and copies ran while one was open for 4% of the time, Pallas kernels for 12%

profile of v2, /device:TPU:8, one launch (start us, length us, event | category | flops | bytes accessed | tf_op | source)
XLA Modules:
  0.0 225.9 jit_solution(2536051901878134737)
XLA Ops:
  5.2 2.3 %heads.2 = (bf16[128,2048]{1,0:T(8,128)(2,1)S(1)}, bf16[48,4096]{1,0:T(8,128)(2,1)S(1)}) custom-call(bf16[1,2,1,128,2048]{4,3,2,1,0:T(8,128)(2,1)S(1)} %copy-done.41, bf16[1,2,1,48,2048]{4,3,2,1,0:T(8,128)(2,1)S(1)} %copy-done.47, bf16[1,2,1,48,2048]{4,3,2,1,0:T(8,128)(2,1)S(1)} %copy-done.49, bf16[1,2,1,128,2048]{4,3,2,1,0:T(8,128)(2,1)S(1)} %copy-done.43), custom_call_target="tpu_custom_call" | custom-call | flops 2000000000 | bytes 3000000 | tf_op jit(solution)/shard_map/heads/pallas_call | solution.py:84
  8.3 3.3 %collective-permute-start.1 = (bf16[48,4096]{1,0:T(8,128)(2,1)S(1)}, bf16[48,4096]{1,0:T(8,128)(2,1)}, u32[]{:S(2)}, u32[]{:S(2)}) collective-permute-start(bf16[48,4096]{1,0:T(8,128)(2,1)S(1)} %get-tuple-element.27.refs_0_), channel_id=1, source_target_pairs={{0,8},{8,16},{16,24},{24,0},{1,9},{9,17},{17,25},{25,1},{2,10},{10... | collective-permute-start | bytes 1179656 | tf_op jit(solution)/shard_map/ppermute | solution.py:319
  11.6 3.0 %collective-permute-start.2 = (bf16[48,4096]{1,0:T(8,128)(2,1)S(1)}, bf16[48,4096]{1,0:T(8,128)(2,1)}, u32[]{:S(2)}, u32[]{:S(2)}) collective-permute-start(bf16[48,4096]{1,0:T(8,128)(2,1)S(1)} %get-tuple-element.27.refs_0_), channel_id=1, source_target_pairs={{0,24},{8,0},{16,8},{24,16},{1,25},{9,1},{17,9},{25,17},{2,26},{10... | collective-permute-start | bytes 1179656 | tf_op jit(solution)/shard_map/ppermute | solution.py:319
  16.0 6.4 %all-to-all-start = ((bf16[8,96,512]{2,1,0:T(8,128)(2,1)}), bf16[8,96,512]{2,1,0:T(8,128)(2,1)S(1)}, u32[]{:S(2)}, u32[]{:S(2)}) async-start(bf16[8,96,512]{2,1,0:T(8,128)(2,1)} %memory.1), calls=%async_computation | async-start | bytes 1572864 | tf_op jit(solution)/shard_map/all_to_all | solution.py:331
  22.4 2.8 %collective-permute-start.21 = (bf16[128,2048]{1,0:T(8,128)(2,1)S(1)}, bf16[128,2048]{1,0:T(8,128)(2,1)S(1)}, u32[]{:S(2)}, u32[]{:S(2)}) collective-permute-start(bf16[128,2048]{1,0:T(8,128)(2,1)S(1)} %bitcast.23), channel_id=1, source_target_pairs={{0,6},{2,0},{4,2},{6,4},{1,7},{3,1},{5,3},{7,5},{8,14},{10,8},{12,... | collective-permute-start | bytes 1572872 | tf_op jit(solution)/shard_map/ppermute | solution.py:319
  26.8 2.8 %collective-permute-start.24 = (bf16[128,2048]{1,0:T(8,128)(2,1)S(1)}, bf16[128,2048]{1,0:T(8,128)(2,1)}, u32[]{:S(2)}, u32[]{:S(2)}) collective-permute-start(bf16[128,2048]{1,0:T(8,128)(2,1)S(1)} %bitcast.27), channel_id=1, source_target_pairs={{0,6},{2,0},{4,2},{6,4},{1,7},{3,1},{5,3},{7,5},{8,14},{10,8},{12,... | collective-permute-start | bytes 1572872 | tf_op jit(solution)/shard_map/ppermute | solution.py:319
  29.6 14.3 %collective-permute-done.2.refs_2_ = bf16[48,4096]{1,0:T(8,128)(2,1)} collective-permute-done((bf16[48,4096]{1,0:T(8,128)(2,1)S(1)}, bf16[48,4096]{1,0:T(8,128)(2,1)}, u32[]{:S(2)}, u32[]{:S(2)}) %collective-permute-start.2) | collective-permute-done | bytes 393248 | tf_op jit(solution)/shard_map/ppermute | solution.py:319
  45.4 4.5 %collective-permute-start.3 = (bf16[48,4096]{1,0:T(8,128)(2,1)}, bf16[48,4096]{1,0:T(8,128)(2,1)}, u32[]{:S(2)}, u32[]{:S(2)}) collective-permute-start(bf16[48,4096]{1,0:T(8,128)(2,1)} %collective-permute-done.1.refs_1_), channel_id=1, source_target_pairs={{0,8},{8,16},{16,24},{24,0},{1,9},{9,17},{17,25},{25,1},{2,10},{10... | collective-permute-start | bytes 1179656 | tf_op jit(solution)/shard_map/ppermute | solution.py:319
  57.7 3.0 %heads.3 = (bf16[128,2048]{1,0:T(8,128)(2,1)S(1)}, bf16[48,4096]{1,0:T(8,128)(2,1)}) custom-call(bf16[1,2,1,128,2048]{4,3,2,1,0:T(8,128)(2,1)S(1)} %copy-done.42, bf16[1,2,1,48,2048]{4,3,2,1,0:T(8,128)(2,1)S(1)} %copy-done.48, bf16[1,2,1,48,2048]{4,3,2,1,0:T(8,128)(2,1)S(1)} %copy-done.50, bf16[1,2,1,128,2048]{4,3,2,1,0:T(8,128)(2,1)S(1)} %copy-done.44), custom_call_target="tpu_custom_call" | custom-call | flops 2000000000 | bytes 3000000 | tf_op jit(solution)/shard_map/heads/pallas_call | solution.py:84
  62.3 4.4 %collective-permute-done.3.refs_3_ = bf16[48,4096]{1,0:T(8,128)(2,1)} collective-permute-done((bf16[48,4096]{1,0:T(8,128)(2,1)}, bf16[48,4096]{1,0:T(8,128)(2,1)}, u32[]{:S(2)}, u32[]{:S(2)}) %collective-permute-start.3) | collective-permute-done | bytes 393248 | tf_op jit(solution)/shard_map/ppermute | solution.py:319
  70.3 13.4 %collective-permute-done.9.refs_10_.refs_2_ = bf16[48,4096]{1,0:T(8,128)(2,1)} collective-permute-done((bf16[48,4096]{1,0:T(8,128)(2,1)}, bf16[48,4096]{1,0:T(8,128)(2,1)}, u32[]{:S(2)}, u32[]{:S(2)}) %collective-permute-start.9) | collective-permute-done | bytes 393248 | tf_op jit(solution)/shard_map/ppermute | solution.py:319
  83.7 3.6 %collective-permute-start.10 = (bf16[48,4096]{1,0:T(8,128)(2,1)}, bf16[48,4096]{1,0:T(8,128)(2,1)}, u32[]{:S(2)}, u32[]{:S(2)}) collective-permute-start(bf16[48,4096]{1,0:T(8,128)(2,1)} %collective-permute-done.9.refs_10_.refs_2_), channel_id=1, source_target_pairs={{0,24},{8,0},{16,8},{24,16},{1,25},{9,1},{17,9},{25,17},{2,26},{10... | collective-permute-start | bytes 1179656 | tf_op jit(solution)/shard_map/ppermute | solution.py:319
  91.7 5.4 %returned.2 = (bf16[8,48,512]{2,1,0:T(8,128)(2,1)S(1)}, f32[8,512]{1,0:T(8,128)S(1)}) custom-call(s32[4]{0:T(128)S(1)} %copy-done.37, bf16[48,4096]{1,0:T(8,128)(2,1)S(1)} %get-tuple-element.27.refs_0_, bf16[48,4096]{1,0:T(8,128)(2,1)} %collective-permute-done.1.refs_1_, bf16[48,4096]{1,0:T(8,128)(2,1)} %collective-permute-done.2.refs_2_, ...), custom_call_target="tpu_custom_call" | custom-call | flops 1610612736 | bytes 8000000 | tf_op jit(solution)/shard_map/returned/pallas_call | solution.py:165
  98.5 5.5 %all-to-all-start.1 = ((bf16[8,48,512]{2,1,0:T(8,128)(2,1)}), bf16[8,48,512]{2,1,0:T(8,128)(2,1)S(1)}, u32[]{:S(2)}, u32[]{:S(2)}) async-start(bf16[8,48,512]{2,1,0:T(8,128)(2,1)} %copy-done.31), calls=%async_computation.1 | async-start | bytes 786432 | tf_op jit(solution)/shard_map/all_to_all | solution.py:331
  109.3 5.1 %returned.3 = (bf16[8,48,512]{2,1,0:T(8,128)(2,1)S(1)}, f32[8,512]{1,0:T(8,128)S(1)}) custom-call(s32[4]{0:T(128)S(1)} %copy-done.38, bf16[48,4096]{1,0:T(8,128)(2,1)} %get-tuple-element.30.refs_8_.refs_0_, bf16[48,4096]{1,0:T(8,128)(2,1)} %collective-permute-done.8.refs_9_.refs_1_, bf16[48,4096]{1,0:T(8,128)(2,1)} %collective-permute-done.9.refs_10_.refs_2_, ...), custom_call_target="tpu_custom_call" | custom-call | flops 1610612736 | bytes 8000000 | tf_op jit(solution)/shard_map/returned/pallas_call | solution.py:165
  118.8 5.8 %all-to-all-start.4 = ((bf16[8,48,512]{2,1,0:T(8,128)(2,1)}), bf16[8,48,512]{2,1,0:T(8,128)(2,1)S(1)}, u32[]{:S(2)}, u32[]{:S(2)}) async-start(bf16[8,48,512]{2,1,0:T(8,128)(2,1)} %copy-done.30), calls=%async_computation.4 | async-start | bytes 786432 | tf_op jit(solution)/shard_map/all_to_all | solution.py:331
  131.6 7.5 %weights.1 = (bf16[128,2048]{1,0:T(8,128)(2,1)S(1)}, bf16[128,2048]{1,0:T(8,128)(2,1)S(1)}, bf16[128,2048]{1,0:T(8,128)(2,1)}, bf16[128,2048]{1,0:T(8,128)(2,1)}...) custom-call(s32[4]{0:T(128)S(1)} %copy-done.39, ...), custom_call_target="tpu_custom_call" | custom-call | flops 3221225472 | bytes 11000000 | tf_op jit(solution)/shard_map/weights/pallas_call | solution.py:211
  141.5 7.9 %collective-permute-start.15 = (bf16[128,2048]{1,0:T(8,128)(2,1)}, bf16[128,2048]{1,0:T(8,128)(2,1)}, u32[]{:S(2)}, u32[]{:S(2)}) collective-permute-start(bf16[128,2048]{1,0:T(8,128)(2,1)} %get-tuple-element.33), channel_id=1, source_target_pairs={{0,2},{2,4},{4,6},{6,0},{1,3},{3,5},{5,7},{7,1},{8,10},{10,12},{12... | collective-permute-start | bytes 1572872 | tf_op jit(solution)/shard_map/ppermute | solution.py:319
  151.7 2.5 %collective-permute-start.28 = (f32[8,512]{1,0:T(8,128)S(1)}, f32[8,512]{1,0:T(8,128)S(1)}, u32[]{:S(2)}, u32[]{:S(2)}) collective-permute-start(f32[8,512]{1,0:T(8,128)S(1)} %add.31), channel_id=1, source_target_pairs={{0,4},{2,6},{4,0},{6,2},{1,5},{3,7},{5,1},{7,3},{8,12},{10,14},{12... | collective-permute-start | bytes 49160 | tf_op jit(solution)/shard_map/ppermute | solution.py:319
  155.4 6.4 %all-to-all-start.2 = ((bf16[8,8,512]{2,1,0:T(8,128)(2,1)}), bf16[8,8,512]{2,1,0:T(8,128)(2,1)S(1)}, u32[]{:S(2)}, u32[]{:S(2)}) async-start(bf16[8,8,512]{2,1,0:T(8,128)(2,1)} %layers.2), calls=%async_computation.2 | async-start | bytes 131072 | tf_op jit(solution)/shard_map/all_to_all | solution.py:331
  161.8 3.3 %collective-permute-done.28 = f32[8,512]{1,0:T(8,128)S(1)} collective-permute-done((f32[8,512]{1,0:T(8,128)S(1)}, f32[8,512]{1,0:T(8,128)S(1)}, u32[]{:S(2)}, u32[]{:S(2)}) %collective-permute-start.28) | collective-permute-done | bytes 16416 | tf_op jit(solution)/shard_map/ppermute | solution.py:319
  166.0 4.3 %all-to-all-done.2.own_ref = bf16[8,8,512]{2,1,0:T(8,128)(2,1)S(1)} async-done(((bf16[8,8,512]{2,1,0:T(8,128)(2,1)}), bf16[8,8,512]{2,1,0:T(8,128)(2,1)S(1)}, u32[]{:S(2)}, u32[]{:S(2)}) %all-to-all-start.2) | async-done | bytes 65568 | tf_op jit(solution)/shard_map/all_to_all | solution.py:331
  170.4 3.3 %all-to-all-start.5 = ((bf16[8,8,512]{2,1,0:T(8,128)(2,1)}), bf16[8,8,512]{2,1,0:T(8,128)(2,1)S(1)}, u32[]{:S(2)}, u32[]{:S(2)}) async-start(bf16[8,8,512]{2,1,0:T(8,128)(2,1)} %layers.3), calls=%async_computation.5 | async-start | bytes 131072 | tf_op jit(solution)/shard_map/all_to_all | solution.py:331
  174.8 3.1 %collective-permute-start = (bf16[1,2,1,128,2048]{4,3,1,2,0:T(8,128)(2,1)}, bf16[1,2,1,128,2048]{4,3,1,2,0:T(8,128)(2,1)}, u32[]{:S(2)}, u32[]{:S(2)}) collective-permute-start(bf16[1,2,1,128,2048]{4,3,1,2,0:T(8,128)(2,1)} %maximum_bitcast_fusion), channel_id=1, source_target_pairs={{32,0},{64,32},{96,64},{128,96},{160,128},{192,160},{224,192},{33,... | collective-permute-start | bytes 3145736 | tf_op jit(solution)/shard_map/ppermute | solution.py:389
  182.0 5.4 %all-to-all-start.3 = ((bf16[8,8,4096]{2,1,0:T(8,128)(2,1)}), bf16[8,8,4096]{2,1,0:T(8,128)(2,1)S(1)}, u32[]{:S(2)}, u32[]{:S(2)}) async-start(bf16[8,8,4096]{2,1,0:T(8,128)(2,1)} %encoder.2), calls=%async_computation.3 | async-start | bytes 1048576 | tf_op jit(solution)/shard_map/all_to_all | solution.py:331
  194.2 3.3 %collective-permute-start.20 = (bf16[128,2048]{1,0:T(8,128)(2,1)S(1)}, bf16[128,2048]{1,0:T(8,128)(2,1)}, u32[]{:S(2)}, u32[]{:S(2)}) collective-permute-start(bf16[128,2048]{1,0:T(8,128)(2,1)S(1)} %add_convert_fusion.1), channel_id=1, source_target_pairs={{0,6},{2,0},{4,2},{6,4},{1,7},{3,1},{5,3},{7,5},{8,14},{10,8},{12,... | collective-permute-start | bytes 1572872 | tf_op jit(solution)/shard_map/ppermute | solution.py:319
  197.5 5.5 %collective-permute-done = bf16[1,2,1,128,2048]{4,3,1,2,0:T(8,128)(2,1)} collective-permute-done((bf16[1,2,1,128,2048]{4,3,1,2,0:T(8,128)(2,1)}, bf16[1,2,1,128,2048]{4,3,1,2,0:T(8,128)(2,1)}, u32[]{:S(2)}, u32[]{:S(2)}) %collective-permute-start) | collective-permute-done | bytes 1048608 | tf_op jit(solution)/shard_map/ppermute | solution.py:389
  204.7 3.4 %all-to-all-done.3.first_ref = bf16[8,8,4096]{2,1,0:T(8,128)(2,1)S(1)} async-done(((bf16[8,8,4096]{2,1,0:T(8,128)(2,1)}), bf16[8,8,4096]{2,1,0:T(8,128)(2,1)S(1)}, u32[]{:S(2)}, u32[]{:S(2)}) %all-to-all-start.3) | async-done | bytes 524320 | tf_op jit(solution)/shard_map/all_to_all | solution.py:331
  208.0 6.1 %all-to-all-start.6 = ((bf16[8,8,4096]{2,1,0:T(8,128)(2,1)}), bf16[8,8,4096]{2,1,0:T(8,128)(2,1)S(1)}, u32[]{:S(2)}, u32[]{:S(2)}) async-start(bf16[8,8,4096]{2,1,0:T(8,128)(2,1)} %encoder.3), calls=%async_computation.6 | async-start | bytes 1048576 | tf_op jit(solution)/shard_map/all_to_all | solution.py:331
  214.2 2.3 %fusion = bf16[1,128,2048]{2,1,0:T(8,128)(2,1)} fusion(bf16[128,2048]{1,0:T(8,128)(2,1)} %collective-permute-done.17, bf16[128,2048]{1,0:T(8,128)(2,1)} %collective-permute-done.16, bf16[128,2048]{1,0:T(8,128)(2,1)S(1)} %copy-done.13), kind=kLoop, calls=%fused_computation.5 | loop fusion | flops 1572864 | bytes 2097152 | tf_op jit(solution)/shard_map/broadcast_in_dim | solution.py:393
  218.7 3.6 %all-to-all-done.6.second_ref = bf16[8,8,4096]{2,1,0:T(8,128)(2,1)S(1)} async-done(((bf16[8,8,4096]{2,1,0:T(8,128)(2,1)}), bf16[8,8,4096]{2,1,0:T(8,128)(2,1)S(1)}, u32[]{:S(2)}, u32[]{:S(2)}) %all-to-all-start.6) | async-done | bytes 524320 | tf_op jit(solution)/shard_map/all_to_all | solution.py:331
  223.6 2.3 %copy.15 = bf16[1,2,1,128,2048]{4,3,2,1,0:T(8,128)(2,1)} copy(bf16[1,2,1,128,2048]{4,3,2,1,0:T(8,128)(2,1)} %bitcast.3) | data formatting | bytes 2097152
  (169 shorter events, 69.0 us)
Async XLA Ops:
  8.3 18.5 %collective-permute-start.1 = (bf16[48,4096]{1,0:T(8,128)(2,1)S(1)}, bf16[48,4096]{1,0:T(8,128)(2,1)}, u32[]{:S(2)}, u32[]{:S(2)}) collective-permute-start(bf16[48,4096]{1,0:T(8,128)(2,1)S(1)} %get-tuple-element.27.refs_0_), channel_id=1, source_target_pairs={{0,8},{8,16},{16,24},{24,0},{1,9},{9,17},{17,25},{25,1},{2,10},{10... | collective-permute-start | bytes 1179656 | tf_op jit(solution)/shard_map/ppermute | solution.py:319
  11.6 32.3 %collective-permute-start.2 = (bf16[48,4096]{1,0:T(8,128)(2,1)S(1)}, bf16[48,4096]{1,0:T(8,128)(2,1)}, u32[]{:S(2)}, u32[]{:S(2)}) collective-permute-start(bf16[48,4096]{1,0:T(8,128)(2,1)S(1)} %get-tuple-element.27.refs_0_), channel_id=1, source_target_pairs={{0,24},{8,0},{16,8},{24,16},{1,25},{9,1},{17,9},{25,17},{2,26},{10... | collective-permute-start | bytes 1179656 | tf_op jit(solution)/shard_map/ppermute | solution.py:319
  16.0 72.0 %all-to-all-start = ((bf16[8,96,512]{2,1,0:T(8,128)(2,1)}), bf16[8,96,512]{2,1,0:T(8,128)(2,1)S(1)}, u32[]{:S(2)}, u32[]{:S(2)}) async-start(bf16[8,96,512]{2,1,0:T(8,128)(2,1)} %memory.1), calls=%async_computation | async-start | bytes 1572864 | tf_op jit(solution)/shard_map/all_to_all | solution.py:331
  22.4 27.5 %collective-permute-start.21 = (bf16[128,2048]{1,0:T(8,128)(2,1)S(1)}, bf16[128,2048]{1,0:T(8,128)(2,1)S(1)}, u32[]{:S(2)}, u32[]{:S(2)}) collective-permute-start(bf16[128,2048]{1,0:T(8,128)(2,1)S(1)} %bitcast.23), channel_id=1, source_target_pairs={{0,6},{2,0},{4,2},{6,4},{1,7},{3,1},{5,3},{7,5},{8,14},{10,8},{12,... | collective-permute-start | bytes 1572872 | tf_op jit(solution)/shard_map/ppermute | solution.py:319
  25.2 20.1 %collective-permute-start.4 = (bf16[48,4096]{1,0:T(8,128)(2,1)S(1)}, bf16[48,4096]{1,0:T(8,128)(2,1)S(1)}, u32[]{:S(2)}, u32[]{:S(2)}) collective-permute-start(bf16[48,4096]{1,0:T(8,128)(2,1)S(1)} %get-tuple-element.27.refs_0_), channel_id=1, source_target_pairs={{0,1},{1,0},{2,3},{3,2},{4,5},{5,4},{6,7},{7,6},{8,9},{9,8},{10,11... | collective-permute-start | bytes 1179656 | tf_op jit(solution)/shard_map/ppermute | solution.py:323
  25.4 24.5 %collective-permute-start.22 = (bf16[128,2048]{1,0:T(8,128)(2,1)S(1)}, bf16[128,2048]{1,0:T(8,128)(2,1)}, u32[]{:S(2)}, u32[]{:S(2)}) collective-permute-start(bf16[128,2048]{1,0:T(8,128)(2,1)S(1)} %bitcast.24), channel_id=1, source_target_pairs={{0,2},{2,4},{4,6},{6,0},{1,3},{3,5},{5,7},{7,1},{8,10},{10,12},{12... | collective-permute-start | bytes 1572872 | tf_op jit(solution)/shard_map/ppermute | solution.py:319
  26.8 24.6 %collective-permute-start.24 = (bf16[128,2048]{1,0:T(8,128)(2,1)S(1)}, bf16[128,2048]{1,0:T(8,128)(2,1)}, u32[]{:S(2)}, u32[]{:S(2)}) collective-permute-start(bf16[128,2048]{1,0:T(8,128)(2,1)S(1)} %bitcast.27), channel_id=1, source_target_pairs={{0,6},{2,0},{4,2},{6,4},{1,7},{3,1},{5,3},{7,5},{8,14},{10,8},{12,... | collective-permute-start | bytes 1572872 | tf_op jit(solution)/shard_map/ppermute | solution.py:319
  43.9 17.6 %collective-permute-start.26 = (bf16[128,2048]{1,0:T(8,128)(2,1)S(1)}, bf16[128,2048]{1,0:T(8,128)(2,1)S(1)}, u32[]{:S(2)}, u32[]{:S(2)}) collective-permute-start(bf16[128,2048]{1,0:T(8,128)(2,1)S(1)} %bitcast.28), channel_id=1, source_target_pairs={{0,2},{2,4},{4,6},{6,0},{1,3},{3,5},{5,7},{7,1},{8,10},{10,12},{12... | collective-permute-start | bytes 1572872 | tf_op jit(solution)/shard_map/ppermute | solution.py:319
  45.4 21.3 %collective-permute-start.3 = (bf16[48,4096]{1,0:T(8,128)(2,1)}, bf16[48,4096]{1,0:T(8,128)(2,1)}, u32[]{:S(2)}, u32[]{:S(2)}) collective-permute-start(bf16[48,4096]{1,0:T(8,128)(2,1)} %collective-permute-done.1.refs_1_), channel_id=1, source_target_pairs={{0,8},{8,16},{16,24},{24,0},{1,9},{9,17},{17,25},{25,1},{2,10},{10... | collective-permute-start | bytes 1179656 | tf_op jit(solution)/shard_map/ppermute | solution.py:319
  49.9 18.9 %collective-permute-start.5 = (bf16[48,4096]{1,0:T(8,128)(2,1)}, bf16[48,4096]{1,0:T(8,128)(2,1)S(1)}, u32[]{:S(2)}, u32[]{:S(2)}) collective-permute-start(bf16[48,4096]{1,0:T(8,128)(2,1)} %collective-permute-done.1.refs_1_), channel_id=1, source_target_pairs={{0,1},{1,0},{2,3},{3,2},{4,5},{5,4},{6,7},{7,6},{8,9},{9,8},{10,11... | collective-permute-start | bytes 1179656 | tf_op jit(solution)/shard_map/ppermute | solution.py:323
  49.9 38.1 %collective-permute-start.23 = (bf16[128,2048]{1,0:T(8,128)(2,1)}, bf16[128,2048]{1,0:T(8,128)(2,1)}, u32[]{:S(2)}, u32[]{:S(2)}) collective-permute-start(bf16[128,2048]{1,0:T(8,128)(2,1)} %collective-permute-done.22.refs_11_), channel_id=1, source_target_pairs={{0,2},{2,4},{4,6},{6,0},{1,3},{3,5},{5,7},{7,1},{8,10},{10,12},{12... | collective-permute-start | bytes 1572872 | tf_op jit(solution)/shard_map/ppermute | solution.py:319
  51.5 36.5 %collective-permute-start.25 = (bf16[128,2048]{1,0:T(8,128)(2,1)}, bf16[128,2048]{1,0:T(8,128)(2,1)}, u32[]{:S(2)}, u32[]{:S(2)}) collective-permute-start(bf16[128,2048]{1,0:T(8,128)(2,1)} %collective-permute-done.24.refs_13_), channel_id=1, source_target_pairs={{0,6},{2,0},{4,2},{6,4},{1,7},{3,1},{5,3},{7,5},{8,14},{10,8},{12,... | collective-permute-start | bytes 1572872 | tf_op jit(solution)/shard_map/ppermute | solution.py:319
  66.6 17.1 %collective-permute-start.9 = (bf16[48,4096]{1,0:T(8,128)(2,1)}, bf16[48,4096]{1,0:T(8,128)(2,1)}, u32[]{:S(2)}, u32[]{:S(2)}) collective-permute-start(bf16[48,4096]{1,0:T(8,128)(2,1)} %get-tuple-element.30.refs_8_.refs_0_), channel_id=1, source_target_pairs={{0,24},{8,0},{16,8},{24,16},{1,25},{9,1},{17,9},{25,17},{2,26},{10... | collective-permute-start | bytes 1179656 | tf_op jit(solution)/shard_map/ppermute | solution.py:319
  69.6 18.4 %collective-permute-start.7 = (bf16[48,4096]{1,0:T(8,128)(2,1)}, bf16[48,4096]{1,0:T(8,128)(2,1)}, u32[]{:S(2)}, u32[]{:S(2)}) collective-permute-start(bf16[48,4096]{1,0:T(8,128)(2,1)} %collective-permute-done.3.refs_3_), channel_id=1, source_target_pairs={{0,1},{1,0},{2,3},{3,2},{4,5},{5,4},{6,7},{7,6},{8,9},{9,8},{10,11... | collective-permute-start | bytes 1179656 | tf_op jit(solution)/shard_map/ppermute | solution.py:323
  69.6 34.9 %collective-permute-start.8 = (bf16[48,4096]{1,0:T(8,128)(2,1)}, bf16[48,4096]{1,0:T(8,128)(2,1)}, u32[]{:S(2)}, u32[]{:S(2)}) collective-permute-start(bf16[48,4096]{1,0:T(8,128)(2,1)} %get-tuple-element.30.refs_8_.refs_0_), channel_id=1, source_target_pairs={{0,8},{8,16},{16,24},{24,0},{1,9},{9,17},{17,25},{25,1},{2,10},{10... | collective-permute-start | bytes 1179656 | tf_op jit(solution)/shard_map/ppermute | solution.py:319
  83.7 20.8 %collective-permute-start.10 = (bf16[48,4096]{1,0:T(8,128)(2,1)}, bf16[48,4096]{1,0:T(8,128)(2,1)}, u32[]{:S(2)}, u32[]{:S(2)}) collective-permute-start(bf16[48,4096]{1,0:T(8,128)(2,1)} %collective-permute-done.9.refs_10_.refs_2_), channel_id=1, source_target_pairs={{0,24},{8,0},{16,8},{24,16},{1,25},{9,1},{17,9},{25,17},{2,26},{10... | collective-permute-start | bytes 1179656 | tf_op jit(solution)/shard_map/ppermute | solution.py:319
  98.5 20.3 %all-to-all-start.1 = ((bf16[8,48,512]{2,1,0:T(8,128)(2,1)}), bf16[8,48,512]{2,1,0:T(8,128)(2,1)S(1)}, u32[]{:S(2)}, u32[]{:S(2)}) async-start(bf16[8,48,512]{2,1,0:T(8,128)(2,1)} %copy-done.31), calls=%async_computation.1 | async-start | bytes 786432 | tf_op jit(solution)/shard_map/all_to_all | solution.py:331
  118.8 36.6 %all-to-all-start.4 = ((bf16[8,48,512]{2,1,0:T(8,128)(2,1)}), bf16[8,48,512]{2,1,0:T(8,128)(2,1)S(1)}, u32[]{:S(2)}, u32[]{:S(2)}) async-start(bf16[8,48,512]{2,1,0:T(8,128)(2,1)} %copy-done.30), calls=%async_computation.4 | async-start | bytes 786432 | tf_op jit(solution)/shard_map/all_to_all | solution.py:331
  141.5 45.9 %collective-permute-start.15 = (bf16[128,2048]{1,0:T(8,128)(2,1)}, bf16[128,2048]{1,0:T(8,128)(2,1)}, u32[]{:S(2)}, u32[]{:S(2)}) collective-permute-start(bf16[128,2048]{1,0:T(8,128)(2,1)} %get-tuple-element.33), channel_id=1, source_target_pairs={{0,2},{2,4},{4,6},{6,0},{1,3},{3,5},{5,7},{7,1},{8,10},{10,12},{12... | collective-permute-start | bytes 1572872 | tf_op jit(solution)/shard_map/ppermute | solution.py:319
  149.5 12.4 %collective-permute-start.29 = (f32[8,512]{1,0:T(8,128)S(1)}, f32[8,512]{1,0:T(8,128)S(1)}, u32[]{:S(2)}, u32[]{:S(2)}) collective-permute-start(f32[8,512]{1,0:T(8,128)S(1)} %add.31), channel_id=1, source_target_pairs={{0,6},{2,0},{4,2},{6,4},{1,7},{3,1},{5,3},{7,5},{8,14},{10,8},{12,... | collective-permute-start | bytes 49160 | tf_op jit(solution)/shard_map/ppermute | solution.py:319
  151.7 13.5 %collective-permute-start.28 = (f32[8,512]{1,0:T(8,128)S(1)}, f32[8,512]{1,0:T(8,128)S(1)}, u32[]{:S(2)}, u32[]{:S(2)}) collective-permute-start(f32[8,512]{1,0:T(8,128)S(1)} %add.31), channel_id=1, source_target_pairs={{0,4},{2,6},{4,0},{6,2},{1,5},{3,7},{5,1},{7,3},{8,12},{10,14},{12... | collective-permute-start | bytes 49160 | tf_op jit(solution)/shard_map/ppermute | solution.py:319
  154.2 11.0 %collective-permute-start.27 = (f32[8,512]{1,0:T(8,128)S(1)}, f32[8,512]{1,0:T(8,128)S(1)}, u32[]{:S(2)}, u32[]{:S(2)}) collective-permute-start(f32[8,512]{1,0:T(8,128)S(1)} %add.31), channel_id=1, source_target_pairs={{0,2},{2,4},{4,6},{6,0},{1,3},{3,5},{5,7},{7,1},{8,10},{10,12},{12... | collective-permute-start | bytes 49160 | tf_op jit(solution)/shard_map/ppermute | solution.py:319
  155.4 14.9 %all-to-all-start.2 = ((bf16[8,8,512]{2,1,0:T(8,128)(2,1)}), bf16[8,8,512]{2,1,0:T(8,128)(2,1)S(1)}, u32[]{:S(2)}, u32[]{:S(2)}) async-start(bf16[8,8,512]{2,1,0:T(8,128)(2,1)} %layers.2), calls=%async_computation.2 | async-start | bytes 131072 | tf_op jit(solution)/shard_map/all_to_all | solution.py:331
  170.4 11.6 %all-to-all-start.5 = ((bf16[8,8,512]{2,1,0:T(8,128)(2,1)}), bf16[8,8,512]{2,1,0:T(8,128)(2,1)S(1)}, u32[]{:S(2)}, u32[]{:S(2)}) async-start(bf16[8,8,512]{2,1,0:T(8,128)(2,1)} %layers.3), calls=%async_computation.5 | async-start | bytes 131072 | tf_op jit(solution)/shard_map/all_to_all | solution.py:331
  174.8 28.2 %collective-permute-start = (bf16[1,2,1,128,2048]{4,3,1,2,0:T(8,128)(2,1)}, bf16[1,2,1,128,2048]{4,3,1,2,0:T(8,128)(2,1)}, u32[]{:S(2)}, u32[]{:S(2)}) collective-permute-start(bf16[1,2,1,128,2048]{4,3,1,2,0:T(8,128)(2,1)} %maximum_bitcast_fusion), channel_id=1, source_target_pairs={{32,0},{64,32},{96,64},{128,96},{160,128},{192,160},{224,192},{33,... | collective-permute-start | bytes 3145736 | tf_op jit(solution)/shard_map/ppermute | solution.py:389
  177.9 15.2 %collective-permute-start.19 = (bf16[128,2048]{1,0:T(8,128)(2,1)}, bf16[128,2048]{1,0:T(8,128)(2,1)}, u32[]{:S(2)}, u32[]{:S(2)}) collective-permute-start(bf16[128,2048]{1,0:T(8,128)(2,1)} %get-tuple-element.38), channel_id=1, source_target_pairs={{0,6},{2,0},{4,2},{6,4},{1,7},{3,1},{5,3},{7,5},{8,14},{10,8},{12,... | collective-permute-start | bytes 1572872 | tf_op jit(solution)/shard_map/ppermute | solution.py:319
  179.9 34.2 %collective-permute-start.17 = (bf16[128,2048]{1,0:T(8,128)(2,1)}, bf16[128,2048]{1,0:T(8,128)(2,1)}, u32[]{:S(2)}, u32[]{:S(2)}) collective-permute-start(bf16[128,2048]{1,0:T(8,128)(2,1)} %get-tuple-element.34), channel_id=1, source_target_pairs={{0,6},{2,0},{4,2},{6,4},{1,7},{3,1},{5,3},{7,5},{8,14},{10,8},{12,... | collective-permute-start | bytes 1572872 | tf_op jit(solution)/shard_map/ppermute | solution.py:319
  182.0 26.1 %all-to-all-start.3 = ((bf16[8,8,4096]{2,1,0:T(8,128)(2,1)}), bf16[8,8,4096]{2,1,0:T(8,128)(2,1)S(1)}, u32[]{:S(2)}, u32[]{:S(2)}) async-start(bf16[8,8,4096]{2,1,0:T(8,128)(2,1)} %encoder.2), calls=%async_computation.3 | async-start | bytes 1048576 | tf_op jit(solution)/shard_map/all_to_all | solution.py:331
  189.4 24.7 %collective-permute-start.16 = (bf16[128,2048]{1,0:T(8,128)(2,1)}, bf16[128,2048]{1,0:T(8,128)(2,1)}, u32[]{:S(2)}, u32[]{:S(2)}) collective-permute-start(bf16[128,2048]{1,0:T(8,128)(2,1)} %add_convert_fusion.3), channel_id=1, source_target_pairs={{0,2},{2,4},{4,6},{6,0},{1,3},{3,5},{5,7},{7,1},{8,10},{10,12},{12... | collective-permute-start | bytes 1572872 | tf_op jit(solution)/shard_map/ppermute | solution.py:319
  191.4 25.1 %collective-permute-start.18 = (bf16[128,2048]{1,0:T(8,128)(2,1)S(1)}, bf16[128,2048]{1,0:T(8,128)(2,1)}, u32[]{:S(2)}, u32[]{:S(2)}) collective-permute-start(bf16[128,2048]{1,0:T(8,128)(2,1)S(1)} %copy-done.46), channel_id=1, source_target_pairs={{0,2},{2,4},{4,6},{6,0},{1,3},{3,5},{5,7},{7,1},{8,10},{10,12},{12... | collective-permute-start | bytes 1572872 | tf_op jit(solution)/shard_map/ppermute | solution.py:319
  194.2 22.2 %collective-permute-start.20 = (bf16[128,2048]{1,0:T(8,128)(2,1)S(1)}, bf16[128,2048]{1,0:T(8,128)(2,1)}, u32[]{:S(2)}, u32[]{:S(2)}) collective-permute-start(bf16[128,2048]{1,0:T(8,128)(2,1)S(1)} %add_convert_fusion.1), channel_id=1, source_target_pairs={{0,6},{2,0},{4,2},{6,4},{1,7},{3,1},{5,3},{7,5},{8,14},{10,8},{12,... | collective-permute-start | bytes 1572872 | tf_op jit(solution)/shard_map/ppermute | solution.py:319
  208.0 14.3 %all-to-all-start.6 = ((bf16[8,8,4096]{2,1,0:T(8,128)(2,1)}), bf16[8,8,4096]{2,1,0:T(8,128)(2,1)S(1)}, u32[]{:S(2)}, u32[]{:S(2)}) async-start(bf16[8,8,4096]{2,1,0:T(8,128)(2,1)} %encoder.3), calls=%async_computation.6 | async-start | bytes 1048576 | tf_op jit(solution)/shard_map/all_to_all | solution.py:331
  (56 other events, 282.6 us)
